TPU v7x, 128 devices: a whole 4x4x4 slice. The times are simulated.
128 devices in a mesh: chain: 8 (over x, z_lo), op: 16 (over y, z_hi, core).
Axes of the slice: x: 4, y: 4, z: 4 (z_hi: 2, z_lo: 2; z = z_hi * 2 + z_lo), core: 2. Of those that a mesh axis runs over, the one named last changes fastest.
Arguments:
- env_in: bfloat16 [16, 16, 128, 128], P('op'), may hold values from -6 to 6
- mps: bfloat16 [8, 4, 16, 128, 128], P('chain'), may hold values from -0.5 to 0.5
- proj: bfloat16 [8, 4, 16, 128, 128], P('chain'), may hold values from -0.5 to 0.5
- mpo: bfloat16 [8, 16, 4, 16, 4], P('chain'), may hold values from -2 to 2
- mpo_charge: int32 [16, 2], replicated, may hold values from -1 to 1
- block_sizes: int32 [9, 16], replicated, may hold values from 32 to 128
Outputs:
- env_out: bfloat16 [8, 16, 16, 128, 128], P('chain', 'op')
All inputs are finite; a program needn't handle non-finite values.
Results may differ from a plain program's by a relative error of at most 0.025.
Values may be sent and summed in bfloat16 or wider, within the bound.
A program may use at most 64 MiB of HBM per device.

v0:
```python
import jax
import jax.numpy as jnp
from jax import lax
from jax.sharding import PartitionSpec as P

MPO_BOND = 16
BLOCK_DIM = 128
UP_VALUES = 8
DOWN_VALUES = 2
SECTORS = 16


UP_CHARGE = (0, 1, 0, 1)
DOWN_CHARGE = (0, 0, 1, 1)


def from_behind(block, axis, distance):
    devices = range(lax.axis_size(axis))
    route = [(i - distance, i) for i in devices if i - distance in devices]
    return lax.ppermute(block, axis, route)


def mask_site(site_mps, site_proj, left_sizes, right_sizes):
    positions = jnp.arange(BLOCK_DIM, dtype=jnp.int32)
    up_index = jnp.arange(UP_VALUES, dtype=jnp.int32)[:, None]
    down_index = jnp.arange(DOWN_VALUES, dtype=jnp.int32)[None, :]
    left_grid = left_sizes.reshape(UP_VALUES, DOWN_VALUES)
    right_grid = jnp.pad(right_sizes.reshape(UP_VALUES, DOWN_VALUES), ((0, 1), (0, 1)))
    mps_grid = site_mps.reshape(4, UP_VALUES, DOWN_VALUES, BLOCK_DIM, BLOCK_DIM)
    proj_grid = site_proj.reshape(4, UP_VALUES, DOWN_VALUES, BLOCK_DIM, BLOCK_DIM)
    mps_parts = []
    proj_parts = []
    for phys_state in range(4):
        up_shift = UP_CHARGE[phys_state]
        down_shift = DOWN_CHARGE[phys_state]
        right_here = right_grid[
            up_shift : up_shift + UP_VALUES, down_shift : down_shift + DOWN_VALUES
        ]
        row_keep = positions[None, None, :] < left_grid[:, :, None]
        column_keep = positions[None, None, :] < right_here[:, :, None]
        keep_mask = row_keep[:, :, :, None] & column_keep[:, :, None, :]
        mps_parts.append(
            jnp.where(keep_mask, mps_grid[phys_state], jnp.zeros_like(mps_grid[phys_state]))
        )
        inside = (up_index + up_shift < UP_VALUES) & (down_index + down_shift < DOWN_VALUES)
        proj_parts.append(
            jnp.where(
                inside[:, :, None, None],
                proj_grid[phys_state],
                jnp.zeros_like(proj_grid[phys_state]),
            )
        )
    return (jnp.stack(mps_parts, axis=0), jnp.stack(proj_parts, axis=0))


def mask_mpo(site_mpo, mpo_charge):
    up_state = jnp.array(UP_CHARGE, dtype=jnp.int32)
    down_state = jnp.array(DOWN_CHARGE, dtype=jnp.int32)
    up_bond = mpo_charge[:, 0]
    down_bond = mpo_charge[:, 1]
    match_up = (
        up_bond[:, None, None, None] + up_state[None, None, None, :]
        == up_state[None, :, None, None] + up_bond[None, None, :, None]
    )
    match_down = (
        down_bond[:, None, None, None] + down_state[None, None, None, :]
        == down_state[None, :, None, None] + down_bond[None, None, :, None]
    )
    return jnp.where(match_up & match_down, site_mpo, jnp.zeros_like(site_mpo))


def mix_row(current, previous, mps_grid, row_index):
    pieces = []
    for phys_state in range(4):
        up_shift = UP_CHARGE[phys_state]
        down_shift = DOWN_CHARGE[phys_state]
        env_row = previous if up_shift else current
        source_row = row_index - up_shift
        mps_row = lax.dynamic_index_in_dim(
            mps_grid[phys_state], jnp.maximum(source_row, 0), 0, keepdims=False
        )
        mps_row = jnp.where(source_row >= 0, mps_row, jnp.zeros_like(mps_row))
        if down_shift:
            env_row = jnp.pad(env_row[:, :-1], ((0, 0), (1, 0), (0, 0), (0, 0)))
            mps_row = jnp.pad(mps_row[:-1], ((1, 0), (0, 0), (0, 0)))
        product = jnp.einsum("wdab,dbc->wdac", env_row, mps_row, preferred_element_type=jnp.float32)
        pieces.append(product.astype(jnp.bfloat16))
    return jnp.stack(pieces, axis=1)


def project_row(mixed_rows, charges, proj_padded, row_index):
    zero_index = jnp.zeros((), jnp.int32)

    def one_bond(inputs):
        mixed_bond, charge_bond = inputs
        term_list = []
        for phys_state in range(4):
            start_up = row_index + 2 - UP_CHARGE[phys_state] + charge_bond[0]
            start_down = 2 - DOWN_CHARGE[phys_state] + charge_bond[1]
            chosen = lax.dynamic_slice(
                proj_padded,
                (zero_index, start_up, start_down, zero_index, zero_index),
                (4, 1, DOWN_VALUES, BLOCK_DIM, BLOCK_DIM),
            )[:, 0]
            one_term = jnp.einsum(
                "tdij,dik->tdjk", chosen, mixed_bond[phys_state], preferred_element_type=jnp.float32
            )
            term_list.append(one_term.astype(jnp.bfloat16))
        return jnp.stack(term_list, axis=0)

    return lax.map(one_bond, (mixed_rows, charges))


def on_device(env_in, mps, proj, mpo, mpo_charge, block_sizes):
    chain_pos = lax.axis_index("chain")
    chain_count = lax.axis_size("chain")
    op_pos = lax.axis_index("op")
    local_bond = env_in.shape[0]
    left_sizes = lax.dynamic_index_in_dim(block_sizes, chain_pos, 0, keepdims=False)
    right_sizes = lax.dynamic_index_in_dim(block_sizes, chain_pos + 1, 0, keepdims=False)
    mps_grid, proj_grid = mask_site(mps[0], proj[0], left_sizes, right_sizes)
    proj_padded = jnp.pad(proj_grid, ((0, 0), (2, 2), (2, 2), (0, 0), (0, 0)))
    mpo_masked = mask_mpo(mpo[0], mpo_charge)
    local_charge = lax.dynamic_slice_in_dim(mpo_charge, op_pos * local_bond, local_bond, 0)
    local_mpo = lax.dynamic_slice_in_dim(mpo_masked, op_pos * local_bond, local_bond, 0)
    flat_local = jnp.transpose(local_mpo, (2, 0, 1, 3)).reshape(MPO_BOND, local_bond * 16)
    env_grid = env_in.reshape(local_bond, UP_VALUES, DOWN_VALUES, BLOCK_DIM, BLOCK_DIM)
    zero_row = jnp.zeros((local_bond, DOWN_VALUES, BLOCK_DIM, BLOCK_DIM), jnp.bfloat16)
    zero_all = jnp.zeros((local_bond, UP_VALUES, DOWN_VALUES, BLOCK_DIM, BLOCK_DIM), jnp.bfloat16)

    def compute_row(current, previous, row_index):
        mixed_rows = mix_row(current, previous, mps_grid, row_index)
        projected = project_row(mixed_rows, local_charge, proj_padded, row_index)
        flat_terms = projected.reshape(local_bond * 16, -1)
        summed = lax.psum_scatter(
            jnp.dot(flat_local, flat_terms, preferred_element_type=jnp.float32),
            "op",
            scatter_dimension=0,
            tiled=True,
        )
        return summed.astype(jnp.bfloat16).reshape(local_bond, DOWN_VALUES, BLOCK_DIM, BLOCK_DIM)

    def advance(step_index, loop_state):
        incoming, previous, collected = loop_state
        row_index = step_index - chain_pos
        active = (row_index >= 0) & (row_index < UP_VALUES)
        row_clipped = jnp.clip(row_index, 0, UP_VALUES - 1)
        first_row = lax.dynamic_index_in_dim(env_grid, row_clipped, 1, keepdims=False)
        first_row = jnp.where(active, first_row, zero_row)
        current = jnp.where(chain_pos == 0, first_row, incoming)
        new_row = compute_row(current, previous, row_clipped)
        new_row = jnp.where(active, new_row, zero_row)
        old_row = lax.dynamic_index_in_dim(collected, row_clipped, 1, keepdims=False)
        collected = lax.dynamic_update_index_in_dim(
            collected, jnp.where(active, new_row, old_row), row_clipped, 1
        )
        incoming = from_behind(new_row, "chain", 1)
        return (incoming, current, collected)

    final_state = lax.fori_loop(
        0, UP_VALUES + chain_count - 1, advance, (zero_row, zero_row, zero_all)
    )
    return final_state[2].reshape(1, local_bond, SECTORS, BLOCK_DIM, BLOCK_DIM)


def solution(mesh):
    return jax.shard_map(
        on_device,
        mesh=mesh,
        in_specs=(
            P("op", None, None, None),
            P("chain", None, None, None, None),
            P("chain", None, None, None, None),
            P("chain", None, None, None, None),
            P(),
            P(),
        ),
        out_specs=P("chain", "op", None, None, None),
        check_vma=False,
    )
```

profile of v0, /device:TPU:39, one launch (start us, length us, event | category | flops | bytes accessed | tf_op | source)
XLA Modules:
  0.0 1474.8 jit_solution(2451044293324837077)
XLA Ops:
  4.1 2.6 and_select_fusion
  9.9 5.9 select_maximum_fusion
  20.1 1454.7 %while.31 = (s32[]{:T(128)}, bf16[1,2,128,128]{3,2,1,0:T(8,128)(2,1)S(1)}, bf16[1,2,128,128]{3,2,1,0:T(8,128)(2,1)S(1)}, bf16[1,8,2,128,128]{4,3,2,1,0:T(8,128)(...) while((s32[]{:T(128)}, ...), condition=%wide.region_2.3_spmd.clone, body=%wide.region_0.2_spmd.clone.sunk | while | flops 179126288 | bytes 16387135 | solution.py:160
  29.8 78.4 %all-reduce.10 = bf16[16,32768]{1,0:T(8,128)(2,1)S(1)} all-reduce(f32[16,32768]{1,0:T(8,128)S(1)} %convolution_bitcast_fusion.2), channel_id=2, replica_groups=mesh['chain'=8,'op'=16] {'op'}, use_global_device_ids=true, to_apply=%region_1.1.clone | all-reduce | flops 524288 | bytes 3145728 | tf_op jit(solution)/shard_map/while
  124.6 79.8 %all-reduce.10 = bf16[16,32768]{1,0:T(8,128)(2,1)S(1)} all-reduce(f32[16,32768]{1,0:T(8,128)S(1)} %convolution_bitcast_fusion.2), channel_id=2, replica_groups=mesh['chain'=8,'op'=16] {'op'}, use_global_device_ids=true, to_apply=%region_1.1.clone | all-reduce | flops 524288 | bytes 3145728 | tf_op jit(solution)/shard_map/while
  208.9 2.7 collective-permute-done
  221.2 79.5 %all-reduce.10 = bf16[16,32768]{1,0:T(8,128)(2,1)S(1)} all-reduce(f32[16,32768]{1,0:T(8,128)S(1)} %convolution_bitcast_fusion.2), channel_id=2, replica_groups=mesh['chain'=8,'op'=16] {'op'}, use_global_device_ids=true, to_apply=%region_1.1.clone | all-reduce | flops 524288 | bytes 3145728 | tf_op jit(solution)/shard_map/while
  305.3 3.4 collective-permute-done
  318.3 80.3 %all-reduce.10 = bf16[16,32768]{1,0:T(8,128)(2,1)S(1)} all-reduce(f32[16,32768]{1,0:T(8,128)S(1)} %convolution_bitcast_fusion.2), channel_id=2, replica_groups=mesh['chain'=8,'op'=16] {'op'}, use_global_device_ids=true, to_apply=%region_1.1.clone | all-reduce | flops 524288 | bytes 3145728 | tf_op jit(solution)/shard_map/while
  403.1 2.7 collective-permute-done
  415.4 79.5 %all-reduce.10 = bf16[16,32768]{1,0:T(8,128)(2,1)S(1)} all-reduce(f32[16,32768]{1,0:T(8,128)S(1)} %convolution_bitcast_fusion.2), channel_id=2, replica_groups=mesh['chain'=8,'op'=16] {'op'}, use_global_device_ids=true, to_apply=%region_1.1.clone | all-reduce | flops 524288 | bytes 3145728 | tf_op jit(solution)/shard_map/while
  499.5 3.4 collective-permute-done
  512.5 79.8 %all-reduce.10 = bf16[16,32768]{1,0:T(8,128)(2,1)S(1)} all-reduce(f32[16,32768]{1,0:T(8,128)S(1)} %convolution_bitcast_fusion.2), channel_id=2, replica_groups=mesh['chain'=8,'op'=16] {'op'}, use_global_device_ids=true, to_apply=%region_1.1.clone | all-reduce | flops 524288 | bytes 3145728 | tf_op jit(solution)/shard_map/while
  596.8 3.2 collective-permute-done
  609.6 79.6 %all-reduce.10 = bf16[16,32768]{1,0:T(8,128)(2,1)S(1)} all-reduce(f32[16,32768]{1,0:T(8,128)S(1)} %convolution_bitcast_fusion.2), channel_id=2, replica_groups=mesh['chain'=8,'op'=16] {'op'}, use_global_device_ids=true, to_apply=%region_1.1.clone | all-reduce | flops 524288 | bytes 3145728 | tf_op jit(solution)/shard_map/while
  693.8 3.3 collective-permute-done
  706.7 79.5 %all-reduce.10 = bf16[16,32768]{1,0:T(8,128)(2,1)S(1)} all-reduce(f32[16,32768]{1,0:T(8,128)S(1)} %convolution_bitcast_fusion.2), channel_id=2, replica_groups=mesh['chain'=8,'op'=16] {'op'}, use_global_device_ids=true, to_apply=%region_1.1.clone | all-reduce | flops 524288 | bytes 3145728 | tf_op jit(solution)/shard_map/while
  790.7 3.5 collective-permute-done
  804.0 79.7 %all-reduce.10 = bf16[16,32768]{1,0:T(8,128)(2,1)S(1)} all-reduce(f32[16,32768]{1,0:T(8,128)S(1)} %convolution_bitcast_fusion.2), channel_id=2, replica_groups=mesh['chain'=8,'op'=16] {'op'}, use_global_device_ids=true, to_apply=%region_1.1.clone | all-reduce | flops 524288 | bytes 3145728 | tf_op jit(solution)/shard_map/while
  888.2 3.3 collective-permute-done
  901.3 79.4 %all-reduce.10 = bf16[16,32768]{1,0:T(8,128)(2,1)S(1)} all-reduce(f32[16,32768]{1,0:T(8,128)S(1)} %convolution_bitcast_fusion.2), channel_id=2, replica_groups=mesh['chain'=8,'op'=16] {'op'}, use_global_device_ids=true, to_apply=%region_1.1.clone | all-reduce | flops 524288 | bytes 3145728 | tf_op jit(solution)/shard_map/while
  985.3 3.4 collective-permute-done
  998.5 80.3 %all-reduce.10 = bf16[16,32768]{1,0:T(8,128)(2,1)S(1)} all-reduce(f32[16,32768]{1,0:T(8,128)S(1)} %convolution_bitcast_fusion.2), channel_id=2, replica_groups=mesh['chain'=8,'op'=16] {'op'}, use_global_device_ids=true, to_apply=%region_1.1.clone | all-reduce | flops 524288 | bytes 3145728 | tf_op jit(solution)/shard_map/while
  1083.4 2.6 collective-permute-done
  1095.8 79.6 %all-reduce.10 = bf16[16,32768]{1,0:T(8,128)(2,1)S(1)} all-reduce(f32[16,32768]{1,0:T(8,128)S(1)} %convolution_bitcast_fusion.2), channel_id=2, replica_groups=mesh['chain'=8,'op'=16] {'op'}, use_global_device_ids=true, to_apply=%region_1.1.clone | all-reduce | flops 524288 | bytes 3145728 | tf_op jit(solution)/shard_map/while
  1179.9 3.2 collective-permute-done
  1192.9 79.4 %all-reduce.10 = bf16[16,32768]{1,0:T(8,128)(2,1)S(1)} all-reduce(f32[16,32768]{1,0:T(8,128)S(1)} %convolution_bitcast_fusion.2), channel_id=2, replica_groups=mesh['chain'=8,'op'=16] {'op'}, use_global_device_ids=true, to_apply=%region_1.1.clone | all-reduce | flops 524288 | bytes 3145728 | tf_op jit(solution)/shard_map/while
  1276.8 3.5 collective-permute-done
  1290.1 79.7 %all-reduce.10 = bf16[16,32768]{1,0:T(8,128)(2,1)S(1)} all-reduce(f32[16,32768]{1,0:T(8,128)S(1)} %convolution_bitcast_fusion.2), channel_id=2, replica_groups=mesh['chain'=8,'op'=16] {'op'}, use_global_device_ids=true, to_apply=%region_1.1.clone | all-reduce | flops 524288 | bytes 3145728 | tf_op jit(solution)/shard_map/while
  1374.4 3.2 collective-permute-done
  1387.4 79.8 %all-reduce.10 = bf16[16,32768]{1,0:T(8,128)(2,1)S(1)} all-reduce(f32[16,32768]{1,0:T(8,128)S(1)} %convolution_bitcast_fusion.2), channel_id=2, replica_groups=mesh['chain'=8,'op'=16] {'op'}, use_global_device_ids=true, to_apply=%region_1.1.clone | all-reduce | flops 524288 | bytes 3145728 | tf_op jit(solution)/shard_map/while
  1471.7 3.1 collective-permute-done
  (297 shorter events, 221.2 us)
Async XLA Ops:
  0.0 6.7 copy-start.1
  0.0 6.8 copy-start.2
  0.0 6.7 copy-start
  7.8 12.3 copy-start.3
  109.9 5.0 collective-permute-start
  206.1 5.5 collective-permute-start
  302.5 6.2 collective-permute-start
  400.3 5.5 collective-permute-start
  496.7 6.1 collective-permute-start
  594.0 6.0 collective-permute-start
  691.0 6.1 collective-permute-start
  787.9 6.3 collective-permute-start
  885.4 6.1 collective-permute-start
  982.5 6.2 collective-permute-start
  1080.6 5.3 collective-permute-start
  1177.1 6.0 collective-permute-start
  1274.0 6.3 collective-permute-start
  1371.6 6.0 collective-permute-start
  1468.9 5.9 collective-permute-start
where the time goes:
time: 1490 us; the launch traced here: 1470 us
  blocking collectives  1190 us (80%)
  matrix products  110 us (7%)
  other arithmetic  63.4 us (4%)
  waiting for transfers between devices  46.6 us (3%)
  local copies, waits for them, and re-layouts  34.4 us (2%)
  starting transfers between devices  19.4 us (1%)
    while x15, blocking collectives  1190 us
    dot_general x60, matrix products, one_bond(): jnp.einsum('tdij,dik->tdjk', chosen, mixed_bond[phys_state], preferred_el...  75.4 us
    ppermute x15, waiting for transfers between devices, from_behind(): return lax.ppermute(block, axis, route)  46.6 us
  transfers between devices with their start and end apart: 15, of which 15 were waited for; matrix products, arithmetic and copies ran while one was open for 2% of the time, Pallas kernels for 0%

commit v1 on v0

v1 whole, which is shorter than its diff:
```python
import jax
import jax.numpy as jnp
from jax import lax
from jax.experimental import pallas as pl
from jax.experimental.pallas import tpu as pltpu
from jax.sharding import PartitionSpec as P

UP_VALUES = 8
DOWN_VALUES = 2
SECTORS = 16
BLOCK = 128
HALF = 64
MESH = pl.DeviceIdType.MESH

UP_CHARGE = (0, 1, 0, 1)
DOWN_CHARGE = (0, 0, 1, 1)
PHYS_ORDER = (0, 2, 1, 3)


def role_of(op):
    return op // 4, (op // 2) % 2, op % 2


def op_of(group, down, half):
    return group * 4 + down * 2 + half


def kernel(charge, coeff, env, mps_rows, proj_cols, out,
           slot, lbuf, mb, own, sib_s, sib_r, part_s, part_r, sbuf, obuf,
           slot_sem, next_ss, init_ss, sib_ss, sib_rs, part_ss, part_rs, out_ss, out_ls, out_rs):
    i = lax.axis_index("chain")
    op = lax.axis_index("op")
    g, d, k = role_of(op)
    me = d * 2 + k
    f32, bf16 = jnp.float32, jnp.bfloat16

    bar = pltpu.get_barrier_semaphore()

    def greet(chain, other):
        pl.semaphore_signal(bar, inc=1, device_id=(chain, other), device_id_type=MESH)

    @pl.when(i > 0)
    def _():
        for gg in range(4):
            greet(i - 1, op_of(gg, d, k))
        for mm in range(4):
            @pl.when(mm != me)
            def _():
                greet(i, op_of(g, mm // 2, mm % 2))

    @pl.when(i == 0)
    def _():
        for other in range(16):
            @pl.when(other != op)
            def _():
                greet(i, other)

    rows = lax.broadcasted_iota(jnp.int32, (1024, 64), 0)
    cols = lax.broadcasted_iota(jnp.int32, (1024, 64), 1)
    spread = jnp.where(rows // 16 == cols, 1.0, 0.0).astype(bf16)
    tall = jnp.dot(spread, coeff[...], preferred_element_type=f32).astype(bf16)
    rows = lax.broadcasted_iota(jnp.int32, (BLOCK, 256), 0)
    cols = lax.broadcasted_iota(jnp.int32, (BLOCK, 256), 1)
    widen = jnp.where(rows == cols // 16, 1.0, 0.0).astype(bf16)
    wide = jnp.dot(tall, widen, preferred_element_type=f32)
    rows = lax.broadcasted_iota(jnp.int32, (1024, 256), 0)
    cols = lax.broadcasted_iota(jnp.int32, (1024, 256), 1)
    mb[...] = jnp.where(rows % 16 == cols % 16, wide, 0.0).astype(bf16)
    lbuf[...] = jnp.zeros_like(lbuf)

    @pl.when(i == 0)
    def _():
        pl.semaphore_wait(bar, 19)

    @pl.when((i > 0) & (i < 7))
    def _():
        pl.semaphore_wait(bar, 7)

    @pl.when(i == 7)
    def _():
        pl.semaphore_wait(bar, 3)

    def init_row(u):
        mine = g * 4 + me
        for other in range(16):
            gg, dd, kk = role_of(other)

            @pl.when(other != op)
            def _():
                pltpu.make_async_remote_copy(
                    env.at[dd, kk, u], slot.at[u, :, mine], init_ss.at[u], slot_sem.at[u],
                    device_id=(i, other), device_id_type=MESH).start()

            @pl.when(other == op)
            def _():
                pltpu.make_async_copy(env.at[dd, kk, u], slot.at[u, :, mine], slot_sem.at[u]).start()

    @pl.when(i == 0)
    def _():
        def two(u, _):
            init_row(u)
            return 0
        lax.fori_loop(0, 2, two, 0)

    def mix(u, first, plane):
        for pair in range(2):
            x = slot[u, pair].reshape(256, 256)
            y = jnp.dot(mb[pl.ds((2 * first + plane) * 256, 256), :], x, preferred_element_type=f32).astype(bf16)
            for side in range(2):
                lbuf[plane, pl.ds((2 * pair + side) * 256, 256), pl.ds(first * BLOCK, BLOCK)] = (
                    y[:, side * BLOCK:(side + 1) * BLOCK])

    def apply(u, plane):
        grown = jnp.dot(lbuf[plane], mps_rows[u, plane], preferred_element_type=f32).astype(bf16)
        grown = grown.reshape(4, 4, HALF, BLOCK)
        for m in range(4):
            up = u + charge[g * 4 + m, 0]
            down = d + plane + charge[g * 4 + m, 1]
            inside = (up >= 0) & (up < UP_VALUES) & (down >= 0) & (down < DOWN_VALUES)
            place = jnp.where(inside, up * 2 + down, SECTORS)
            res = jnp.dot(proj_cols[place], grown[:, m].reshape(256, BLOCK), preferred_element_type=f32)
            own[plane, m] = res[:HALF]
            sib_s[u, plane, m] = res[HALF:].astype(bf16)

    def sibling(u, plane):
        return pltpu.make_async_remote_copy(
            sib_s.at[u, plane], sib_r.at[u, plane], sib_ss.at[u, plane], sib_rs.at[u, plane],
            device_id=(i, op_of(g, d, 1 - k)), device_id_type=MESH)

    def partial(u):
        return pltpu.make_async_remote_copy(
            part_s.at[u], part_r.at[u], part_ss.at[u], part_rs.at[u],
            device_id=(i, op_of(g, 1 - d, k)), device_id_type=MESH)

    def step(u, _):
        @pl.when((i == 0) & (u < 6))
        def _():
            init_row(u + 2)
        pltpu.make_async_copy(slot.at[u], slot.at[u], slot_sem.at[u]).wait()
        mix(u, 0, 0)
        apply(u, 0)
        sibling(u, 0).start()

        @pl.when(d == 0)
        def _():
            mix(u, 0, 1)
            apply(u, 1)
            sibling(u, 1).start()

        @pl.when(d == 1)
        def _():
            mix(u, 1, 0)
        sibling(u, 0).wait_recv()

        @pl.when(d == 1)
        def _():
            partial(u).wait_recv()
            for m in range(4):
                own[0, m] = own[0, m] + part_r[u, m].astype(f32)

        for m in range(4):
            res = (own[0, m] + sib_r[u, 0, m].astype(f32)).astype(bf16)
            obuf[u, m] = res
            for pair in range(2):
                for side in range(2):
                    start = pair * 32 + side * 16
                    sbuf[u, pair, m, :, pl.ds(side * BLOCK, BLOCK)] = res[start:start + 16]

        @pl.when(i < 7)
        def _():
            for gg in range(4):
                pltpu.make_async_remote_copy(
                    sbuf.at[u], slot.at[u, :, pl.ds(g * 4, 4)], next_ss.at[u], slot_sem.at[u],
                    device_id=(i + 1, op_of(gg, d, k)), device_id_type=MESH).start()

        @pl.when(d == 0)
        def _():
            sibling(u, 1).wait_recv()
            for m in range(4):
                part_s[u, m] = (own[1, m] + sib_r[u, 1, m].astype(f32)).astype(bf16)
            partial(u).start()

        for m in range(4):
            dst = out.at[u * 2 + d, pl.ds(k * HALF, HALF)]

            @pl.when(m != me)
            def _():
                pltpu.make_async_remote_copy(
                    obuf.at[u, m], dst, out_ss.at[u], out_rs,
                    device_id=(i, op_of(g, m // 2, m % 2)), device_id_type=MESH).start()

            @pl.when(m == me)
            def _():
                pltpu.make_async_copy(obuf.at[u, m], dst, out_ls.at[u]).start()

        @pl.when(d == 0)
        def _():
            mix(u, 1, 0)
            mix(u, 1, 1)
        return 0

    lax.fori_loop(0, UP_VALUES, step, 0)

    def drain(u, _):
        @pl.when(i == 0)
        def _():
            part = slot.at[u, :, pl.ds(0, 15)]
            pltpu.make_async_copy(part, part, init_ss.at[u]).wait()

        @pl.when(i < 7)
        def _():
            pltpu.make_async_copy(slot.at[u], slot.at[u], next_ss.at[u]).wait()
        sibling(u, 0).wait_send()

        @pl.when(d == 0)
        def _():
            sibling(u, 1).wait_send()
            partial(u).wait_send()
        three = obuf.at[u, pl.ds(0, 3)]
        pltpu.make_async_copy(three, three, out_ss.at[u]).wait()
        pltpu.make_async_copy(obuf.at[u, 0], obuf.at[u, 0], out_ls.at[u]).wait()
        return 0

    lax.fori_loop(0, UP_VALUES, drain, 0)
    pltpu.make_async_copy(out.at[pl.ds(0, 12)], out.at[pl.ds(0, 12)], out_rs).wait()


def mask_mpo(site_mpo, mpo_charge):
    up_state = jnp.array(UP_CHARGE, dtype=jnp.int32)
    down_state = jnp.array(DOWN_CHARGE, dtype=jnp.int32)
    up_bond = mpo_charge[:, 0]
    down_bond = mpo_charge[:, 1]
    match_up = (
        up_bond[:, None, None, None] + up_state[None, None, None, :]
        == up_state[None, :, None, None] + up_bond[None, None, :, None]
    )
    match_down = (
        down_bond[:, None, None, None] + down_state[None, None, None, :]
        == down_state[None, :, None, None] + down_bond[None, None, :, None]
    )
    return jnp.where(match_up & match_down, site_mpo, jnp.zeros_like(site_mpo))


def on_device(env_in, mps, proj, mpo, mpo_charge, block_sizes):
    i = lax.axis_index("chain")
    g, d, k = role_of(lax.axis_index("op"))
    bf16 = jnp.bfloat16

    masked = mask_mpo(mpo[0], mpo_charge)
    charge = mpo_charge
    mine = lax.dynamic_slice_in_dim(masked, g * 4, 4, 2)
    coeff = jnp.stack([mine[:, p] for p in PHYS_ORDER], axis=0).transpose(0, 2, 3, 1).reshape(64, 16)
    coeff = jnp.pad(coeff, ((0, 0), (0, BLOCK - 16)))

    left = lax.dynamic_index_in_dim(block_sizes, i, 0, keepdims=False).reshape(UP_VALUES, DOWN_VALUES)
    right = lax.dynamic_index_in_dim(block_sizes, i + 1, 0, keepdims=False).reshape(UP_VALUES, DOWN_VALUES)
    right = jnp.pad(right, ((0, 1), (0, 1)))
    left = lax.dynamic_index_in_dim(left, d, 1, keepdims=False)
    right_same = lax.dynamic_index_in_dim(right, d, 1, keepdims=False)
    right_more = lax.dynamic_index_in_dim(right, d + 1, 1, keepdims=False)
    grid = lax.dynamic_index_in_dim(mps[0].reshape(4, UP_VALUES, DOWN_VALUES, BLOCK, BLOCK), d, 2, keepdims=False)
    pos = jnp.arange(BLOCK, dtype=jnp.int32)
    planes = []
    for p in range(4):
        r = right_more if DOWN_CHARGE[p] else right_same
        r = r[UP_CHARGE[p]:UP_CHARGE[p] + UP_VALUES]
        keep = (pos[None, :, None] < left[:, None, None]) & (pos[None, None, :] < r[:, None, None])
        block = jnp.where(keep, grid[p], jnp.zeros_like(grid[p]))
        if UP_CHARGE[p]:
            block = jnp.pad(block[:-1], ((1, 0), (0, 0), (0, 0)))
        planes.append(block)
    mps_rows = jnp.stack(planes, axis=1).reshape(UP_VALUES, 2, 256, BLOCK)

    pgrid = lax.dynamic_slice_in_dim(proj[0].reshape(4, UP_VALUES, DOWN_VALUES, BLOCK, BLOCK), k * HALF, HALF, 3)
    parts = []
    for t in range(4):
        up, down = UP_CHARGE[t], DOWN_CHARGE[t]
        part = pgrid[t][:UP_VALUES - up, :DOWN_VALUES - down]
        parts.append(jnp.pad(part, ((up, 0), (down, 0), (0, 0), (0, 0))))
    stacked = jnp.stack(parts, axis=2).reshape(SECTORS, 4, 4, 16, 2, HALF)
    stacked = jnp.where(k == 0, stacked, stacked[:, :, :, :, ::-1])
    proj_cols = stacked.transpose(0, 4, 5, 2, 1, 3).reshape(SECTORS, BLOCK, 256)
    proj_cols = jnp.pad(proj_cols, ((0, 1), (0, 0), (0, 0)))

    env = env_in[0].reshape(UP_VALUES, 2, 2, 2, 2, 16, BLOCK).transpose(1, 2, 0, 3, 5, 4, 6)
    env = env.reshape(2, 2, UP_VALUES, 2, 16, 256)

    vm = pl.BlockSpec(memory_space=pltpu.VMEM)
    dma = pltpu.SemaphoreType.DMA
    out = pl.pallas_call(
        kernel,
        out_shape=jax.ShapeDtypeStruct((SECTORS, BLOCK, BLOCK), bf16),
        in_specs=[pl.BlockSpec(memory_space=pltpu.SMEM), vm, vm, vm, vm],
        out_specs=pl.BlockSpec(memory_space=pl.ANY),
        scratch_shapes=[
            pltpu.VMEM((UP_VALUES, 2, 16, 16, 256), bf16),
            pltpu.VMEM((2, 1024, 256), bf16),
            pltpu.VMEM((1024, 256), bf16),
            pltpu.VMEM((2, 4, HALF, BLOCK), jnp.float32),
            pltpu.VMEM((UP_VALUES, 2, 4, HALF, BLOCK), bf16),
            pltpu.VMEM((UP_VALUES, 2, 4, HALF, BLOCK), bf16),
            pltpu.VMEM((UP_VALUES, 4, HALF, BLOCK), bf16),
            pltpu.VMEM((UP_VALUES, 4, HALF, BLOCK), bf16),
            pltpu.VMEM((UP_VALUES, 2, 4, 16, 256), bf16),
            pltpu.VMEM((UP_VALUES, 4, HALF, BLOCK), bf16),
            dma((8,)), dma((8,)), dma((8,)), dma((8, 2)), dma((8, 2)), dma((8,)), dma((8,)), dma((8,)), dma((8,)), dma,
        ],
        compiler_params=pltpu.CompilerParams(collective_id=0, has_side_effects=True, vmem_limit_bytes=40 << 20),
        name="sweep",
    )(charge, coeff, env, mps_rows, proj_cols)
    return out[None, None]


def solution(mesh):
    return jax.shard_map(
        on_device,
        mesh=mesh,
        in_specs=(
            P("op", None, None, None),
            P("chain", None, None, None, None),
            P("chain", None, None, None, None),
            P("chain", None, None, None, None),
            P(),
            P(),
        ),
        out_specs=P("chain", "op", None, None, None),
        check_vma=False,
    )
```

time: 1490 us -> 249 us (0.17); the launches traced: 1470 us -> 249 us
  blocking collectives: 1190 us -> 0 us
  Pallas kernels: 0 us -> 212 us
  matrix products: 110 us -> 0 us
  other arithmetic: 63.4 us -> 5.94 us
  waiting for transfers between devices: 46.6 us -> 0 us
  starting transfers between devices: 19.4 us -> 0 us
    while x15 -> x0, blocking collectives: 1190 us -> none
    pallas_call x0 -> x1, Pallas kernels: none -> 212 us  [on_device(): pl.pallas_call(kernel, out_shape=jax.ShapeDtypeStruct((SECTORS, BLOCK, BL...]
    dot_general x105 -> x0, matrix products: 110 us -> none  [the longest x60 75.4 us: one_bond(): jnp.einsum('tdij,dik->tdjk', chosen, mixed_bond[phys_state], preferred_el...]
    ppermute x15 -> x0, waiting for transfers between devices: 46.6 us -> none  [from_behind(): return lax.ppermute(block, axis, route)]
    select_n x33 -> x2, other arithmetic: 31.6 us -> 1.51 us  [on_device(): block = jnp.where(keep, grid[p], jnp.zeros_like(grid[p]))]
    dynamic_update_slice x15 -> x0, other arithmetic: 22.4 us -> none  [advance(): lax.dynamic_update_index_in_dim(collected, jnp.where(active, new_row, old...]
    ppermute x15 -> x0, starting transfers between devices: 19.4 us -> none  [from_behind(): return lax.ppermute(block, axis, route)]
    rev x0 -> x1, local copies, waits for them, and re-layouts: none -> 15.2 us  [on_device(): stacked = jnp.where(k == 0, stacked, stacked[:, :, :, :, ::-1])]
  transfers between devices with their start and end apart: 15 -> 0, of which waited for: 15 -> 0; matrix products, arithmetic and copies ran while one was open for 2% -> 0% of each run, Pallas kernels for 0% -> 0%
where the time goes in v1:
time: 249 us
  Pallas kernels  212 us (85%)
  local copies, waits for them, and re-layouts  30.5 us (12%)
  other arithmetic  5.94 us (2%)
    pallas_call x1, Pallas kernels, on_device(): pl.pallas_call(kernel, out_shape=jax.ShapeDtypeStruct((SECTORS, BLOCK, BL...  212 us
    rev x1, local copies, waits for them, and re-layouts, on_device(): stacked = jnp.where(k == 0, stacked, stacked[:, :, :, :, ::-1])  15.2 us

profile of v1, /device:TPU:39, one launch (start us, length us, event | category | flops | bytes accessed | tf_op | source)
XLA Modules:
  0.0 249.1 jit_solution(18363803796156186367)
XLA Ops:
  0.0 1.9 dynamic-slice_bitcast_fusion
  1.9 0.2 stack.33
  2.1 0.4 constant_dynamic-update-slice_fusion.3
  2.6 1.0 dynamic-slice_bitcast_fusion.6
  3.6 0.2 stack.34
  3.8 0.5 constant_dynamic-update-slice_fusion.2
  4.4 0.2 stack.35
  4.6 0.5 constant_dynamic-update-slice_fusion.1
  5.1 0.9 slice.113
  6.1 0.2 stack.36
  6.3 0.5 constant_dynamic-update-slice_fusion
  6.8 15.2 %rev.3 = bf16[16,4,4,16,2,64]{5,4,3,2,0,1:T(2,128)(2,1)} reverse(bf16[16,4,4,16,2,64]{5,4,3,2,0,1:T(2,128)(2,1)S(1)} %constant_dynamic-update-slice_fusion), dimensions={4} | reverse | bytes 2097152 | tf_op jit(solution)/shard_map/rev | solution.py:281
  22.0 3.8 %fusion = bf16[16,2,64,4,4,16]{2,1,5,3,0,4:T(2,128)(2,1)S(1)} fusion(bf16[16,4,4,16,2,64]{5,4,3,2,0,1:T(2,128)(2,1)S(1)} %constant_dynamic-update-slice_fusion, bf16[16,4,4,16,2,64]{5,4,3,2,0,1:T(2,128)(2,1)} %rev.3, pred[]{:T(512)S(6)} %eq.38), kind=kLoop, calls=%fused_computation.1 | loop fusion | flops 524288 | bytes 3145729 | tf_op jit(solution)/shard_map/transpose | solution.py:282
  25.7 2.4 copy.41
  28.2 1.0 reshape.328
  29.2 0.5 copy.42
  29.7 0.1 pad.38.proj_cols
  29.8 0.7 fusion.7
  30.6 0.2 fusion.5
  31.1 0.2 dynamic-slice_reduce_fusion
  31.4 1.3 fusion.1
  32.7 1.1 dynamic-slice_bitcast_fusion.4
  33.8 0.2 and_select_fusion.3
  34.1 0.1 pad_maximum_fusion
  34.3 0.2 copy-done.2
  34.7 0.1 copy.35
  34.9 0.1 and_select_fusion.4
  35.1 0.5 copy.50
  35.6 0.3 reshape.324.env
  35.9 0.1 copy.43.charge
  36.0 212.3 %sweep.1 = bf16[16,128,128]{2,1,0:T(8,128)(2,1)S(1)} custom-call(s32[16,2]{1,0:T(8,128)S(1)} %copy.43.charge, bf16[64,128]{1,0:T(8,128)(2,1)S(1)} %pad.31.coeff, bf16[2,2,8,2,16,256]{5,4,3,2,1,0:T(8,128)(2,1)S(1)} %reshape.324.env, bf16[8,2,256,128]{3,2,1,0:T(8,128)(2,1)S(1)} %bitcast.76, bf16[17,128,256]{2,1,0:T(8,128)(2,1)S(1)} %pad.38.proj_cols), custom_call_target="tpu_custom_call" | custom-call | tf_op jit(solution)/shard_map/sweep/pallas_call | solution.py:290
  248.3 0.8 copy.55
  (28 shorter events, 0.9 us)
Async XLA Ops:
  33.8 0.7 copy-start.2
  33.8 0.7 copy-start.3
  33.8 0.7 copy-start.4
  33.8 0.9 copy-start.1
  33.8 1.3 copy-start

commit v2 on v1

v2 whole, which is shorter than its diff:
```python
import jax
import jax.numpy as jnp
from jax import lax
from jax.experimental import pallas as pl
from jax.experimental.pallas import tpu as pltpu
from jax.sharding import PartitionSpec as P

UP_VALUES = 8
DOWN_VALUES = 2
SECTORS = 16
BLOCK = 128
HALF = 64
AHEAD = 3
MESH = pl.DeviceIdType.MESH

UP_CHARGE = (0, 1, 0, 1)
DOWN_CHARGE = (0, 0, 1, 1)
PHYS_ORDER = (0, 2, 1, 3)


def role_of(op):
    y = op // 4
    return (op // 2) % 2 * 2 + y % 2, y // 2, op % 2


def op_of(group, down, half):
    return (down * 2 + group % 2) * 4 + group // 2 * 2 + half


def bond_of(group, member):
    return op_of(group, member // 2, member % 2)


def kernel(charge, sizes, coeff, env, mps, proj, out,
           slot, lbuf, mb, own, sib_s, sib_r, part_s, part_r, sbuf, obuf, env_r, mrows, pcols,
           slot_sem, next_ss, init_ss, sib_ss, sib_rs, part_ss, part_rs, out_ss, out_ls, load_sem, out_rs):
    i = lax.axis_index("chain")
    op = lax.axis_index("op")
    g, d, k = role_of(op)
    me = d * 2 + k
    f32, bf16 = jnp.float32, jnp.bfloat16

    bar = pltpu.get_barrier_semaphore()

    def greet(chain, group, down, half):
        pl.semaphore_signal(bar, inc=1, device_id=(chain, op_of(group, down, half)), device_id_type=MESH)

    @pl.when(i > 0)
    def _():
        for j in range(4):
            greet(i - 1, (g + j) % 4, d, k)

    @pl.when(i == 0)
    def _():
        for j in range(8):
            greet(1, (g + j // 2) % 4, 1 - d, (k + j) % 2)
        for j in range(2, 8):
            greet(0, (g + j // 2) % 4, d, (k + j) % 2)
    greet(i, g, d, 1 - k)
    greet(i, g, 1 - d, k)
    greet(i, g, 1 - d, 1 - k)

    target_down = (d + i) % 2

    def env_load(half, side):
        return pltpu.make_async_copy(
            env.at[:, target_down, half, :, side], env_r.at[half, :, :, :, pl.ds(side * BLOCK, BLOCK)], load_sem.at[0])

    @pl.when(i < 2)
    def _():
        for half in range(2):
            for side in range(2):
                env_load(half, side).start()

    def mps_load(p):
        up = UP_CHARGE[p]
        return pltpu.make_async_copy(
            mps.at[p, pl.ds(0, UP_VALUES - up), d], mrows.at[pl.ds(up, UP_VALUES - up), p // 2, up], load_sem.at[1 + p])

    def proj_load(t):
        up, down = UP_CHARGE[t], DOWN_CHARGE[t]
        return pltpu.make_async_copy(
            proj.at[t, pl.ds(0, UP_VALUES - up), pl.ds(0, DOWN_VALUES - down), pl.ds(k * HALF, HALF)],
            pcols.at[pl.ds(up, UP_VALUES - up), pl.ds(down, DOWN_VALUES - down), t], load_sem.at[5 + t])
    for p in range(4):
        mps_load(p).start()
        proj_load(p).start()
    zero = jnp.zeros((HALF, BLOCK), bf16)
    for t in range(4):
        pcols[UP_VALUES, 0, t] = zero
        for down in range(2):
            if UP_CHARGE[t]:
                pcols[0, down, t] = zero
        if DOWN_CHARGE[t]:
            for up in range(UP_CHARGE[t], UP_VALUES):
                pcols[up, 0, t] = zero
    for plane in range(2):
        mrows[0, plane, 1] = jnp.zeros((BLOCK, BLOCK), bf16)
    lbuf[...] = jnp.zeros_like(lbuf)

    rows = lax.broadcasted_iota(jnp.int32, (16, 64), 0)
    cols = lax.broadcasted_iota(jnp.int32, (16, 64), 1)
    pick = jnp.where(cols == bond_of(g, rows // 4) * 4 + rows % 4, 1.0, 0.0).astype(bf16)
    mine = lax.dot_general(pick, coeff[...], (((1,), (1,)), ((), ())), preferred_element_type=f32).astype(bf16)
    rows = lax.broadcasted_iota(jnp.int32, (16, 256), 0)
    cols = lax.broadcasted_iota(jnp.int32, (16, 256), 1)
    col_up = jnp.zeros((16, 256), jnp.int32)
    col_down = jnp.zeros((16, 256), jnp.int32)
    row_up = -(rows % 2)
    row_down = -((rows // 2) % 2)
    for n in range(16):
        b = bond_of(n // 4, n % 4)
        col_up = jnp.where(cols // 16 == n, charge[b, 0], col_up)
        col_down = jnp.where(cols // 16 == n, charge[b, 1], col_down)
    for m in range(4):
        b = bond_of(g, m)
        row_up = row_up + jnp.where(rows // 4 == m, charge[b, 0], 0)
        row_down = row_down + jnp.where(rows // 4 == m, charge[b, 1], 0)
    rows = lax.broadcasted_iota(jnp.int32, (64, 256), 0)
    cols = lax.broadcasted_iota(jnp.int32, (64, 256), 1)
    slot_bond = bond_of(cols // 64, cols // 16 % 4)
    long_rows = lax.broadcasted_iota(jnp.int32, (256, 256), 0)
    long_cols = lax.broadcasted_iota(jnp.int32, (256, 256), 1)
    repeat = jnp.where(
        lax.broadcasted_iota(jnp.int32, (256, 16), 0) // 16 == lax.broadcasted_iota(jnp.int32, (256, 16), 1),
        1.0, 0.0).astype(bf16)
    for place, p in enumerate(PHYS_ORDER):
        widen = jnp.where(rows == slot_bond * 4 + p, 1.0, 0.0).astype(bf16)
        wide = jnp.dot(mine, widen, preferred_element_type=f32)
        match = (col_up == row_up + UP_CHARGE[p]) & (col_down == row_down + DOWN_CHARGE[p])
        wide = jnp.where(match, wide, 0.0).astype(bf16)
        tall = jnp.dot(repeat, wide, preferred_element_type=f32)
        mb[place * 256:(place + 1) * 256, :] = jnp.where(long_rows % 16 == long_cols % 16, tall, 0.0).astype(bf16)

    @pl.when(i == 0)
    def _():
        pl.semaphore_wait(bar, 13)

    @pl.when(i == 1)
    def _():
        pl.semaphore_wait(bar, 15)

    @pl.when((i > 1) & (i < 7))
    def _():
        pl.semaphore_wait(bar, 7)

    @pl.when(i == 7)
    def _():
        pl.semaphore_wait(bar, 3)

    place = g * 4 + me

    def init_row(u, first):
        for j in range(first, 8):
            half = (k + j) % 2
            pltpu.make_async_remote_copy(
                env_r.at[half, u], slot.at[u, :, place], init_ss.at[u], slot_sem.at[u],
                device_id=(0, op_of((g + j // 2) % 4, target_down, half)), device_id_type=MESH).start()

    def init_own(u):
        init_row(u, 1)
        pltpu.make_async_copy(env_r.at[k, u], slot.at[u, :, place], slot_sem.at[u]).start()

    @pl.when(i < 2)
    def _():
        pltpu.make_async_copy(env_r, env_r, load_sem.at[0]).wait()

    @pl.when(i == 0)
    def _():
        def start(u, _):
            init_own(u)
            return 0
        lax.fori_loop(0, AHEAD, start, 0)

    @pl.when(i == 1)
    def _():
        def start(u, _):
            init_row(u, 0)
            return 0
        lax.fori_loop(0, UP_VALUES, start, 0)

    for p in range(4):
        mps_load(p).wait()
    rows = lax.broadcasted_iota(jnp.int32, (BLOCK, BLOCK), 0)
    cols = lax.broadcasted_iota(jnp.int32, (BLOCK, BLOCK), 1)

    def mask_row(u, _):
        for plane in range(2):
            for up in range(2):
                left = sizes[i, jnp.maximum(u - up, 0) * 2 + d]
                right = sizes[i + 1, u * 2 + jnp.minimum(d + plane, 1)]
                keep = (rows < left) & (cols < right)
                mrows[u, plane, up] = jnp.where(keep, mrows[u, plane, up].astype(f32), 0.0).astype(bf16)
        return 0
    lax.fori_loop(0, UP_VALUES, mask_row, 0)
    for t in range(4):
        proj_load(t).wait()

    def mix(u, first, planes):
        for pair in range(2):
            x = slot[u, pair].reshape(256, 256)
            y = jnp.dot(mb[first * 512:first * 512 + planes * 256, :], x, preferred_element_type=f32).astype(bf16)
            for side in range(2):
                for plane in range(planes):
                    lbuf[plane, pl.ds((2 * pair + side) * 256, 256), pl.ds(first * BLOCK, BLOCK)] = (
                        y[plane * 256:(plane + 1) * 256, side * BLOCK:(side + 1) * BLOCK])

    def apply(u, plane):
        grown = jnp.dot(lbuf[plane], mrows[u, plane].reshape(256, BLOCK), preferred_element_type=f32).astype(bf16)
        for m in range(4):
            b = bond_of(g, m)
            up = u + charge[b, 0]
            down = d + plane + charge[b, 1]
            inside = (up >= 0) & (up < UP_VALUES) & (down >= 0) & (down < DOWN_VALUES)
            up = jnp.where(inside, up, UP_VALUES)
            down = jnp.where(inside, down, 0)
            piece = jnp.concatenate(
                [grown[at * 256 + m * 64 + t * 16:at * 256 + m * 64 + t * 16 + 16] for t in range(4) for at in range(4)], axis=0)
            res = lax.dot_general(pcols[up, down].reshape(256, BLOCK), piece, (((0,), (0,)), ((), ())),
                                  preferred_element_type=f32)
            own[plane, m] = jnp.where(k == 0, res[:HALF], res[HALF:])
            sib_s[u, plane, m] = jnp.where(k == 0, res[HALF:], res[:HALF]).astype(bf16)

    def sibling(u, plane):
        return pltpu.make_async_remote_copy(
            sib_s.at[u, plane], sib_r.at[u, plane], sib_ss.at[u, plane], sib_rs.at[u, plane],
            device_id=(i, op_of(g, d, 1 - k)), device_id_type=MESH)

    def partial(u):
        return pltpu.make_async_remote_copy(
            part_s.at[u], part_r.at[u], part_ss.at[u], part_rs.at[u],
            device_id=(i, op_of(g, 1 - d, k)), device_id_type=MESH)

    def step(u, _):
        @pl.when((i == 0) & (u < UP_VALUES - AHEAD))
        def _():
            init_own(u + AHEAD)
        pltpu.make_async_copy(slot.at[u], slot.at[u], slot_sem.at[u]).wait()

        @pl.when(d == 0)
        def _():
            mix(u, 0, 2)

        @pl.when(d == 1)
        def _():
            mix(u, 0, 1)
        apply(u, 0)
        sibling(u, 0).start()

        @pl.when(d == 0)
        def _():
            apply(u, 1)
            sibling(u, 1).start()

        @pl.when(d == 1)
        def _():
            mix(u, 1, 1)
        sibling(u, 0).wait_recv()

        @pl.when(d == 1)
        def _():
            partial(u).wait_recv()
            for m in range(4):
                own[0, m] = own[0, m] + part_r[u, m].astype(f32)

        for m in range(4):
            res = (own[0, m] + sib_r[u, 0, m].astype(f32)).astype(bf16)
            obuf[u, m] = res
            for pair in range(2):
                for side in range(2):
                    start = pair * 32 + side * 16
                    sbuf[u, pair, m, :, pl.ds(side * BLOCK, BLOCK)] = res[start:start + 16]

        @pl.when(i < 7)
        def _():
            for j in range(4):
                pltpu.make_async_remote_copy(
                    sbuf.at[u], slot.at[u, :, pl.ds(g * 4, 4)], next_ss.at[u], slot_sem.at[u],
                    device_id=(i + 1, op_of((g + j) % 4, d, k)), device_id_type=MESH).start()

        @pl.when(d == 0)
        def _():
            sibling(u, 1).wait_recv()
            for m in range(4):
                part_s[u, m] = (own[1, m] + sib_r[u, 1, m].astype(f32)).astype(bf16)
            partial(u).start()

        dst = out.at[u * 2 + d, pl.ds(k * HALF, HALF)]
        for j in range(1, 4):
            m = (me + j) % 4
            pltpu.make_async_remote_copy(
                obuf.at[u, m], dst, out_ss.at[u], out_rs,
                device_id=(i, bond_of(g, m)), device_id_type=MESH).start()
        pltpu.make_async_copy(obuf.at[u, me], dst, out_ls.at[u]).start()

        @pl.when(d == 0)
        def _():
            mix(u, 1, 2)
        return 0

    lax.fori_loop(0, UP_VALUES, step, 0)

    def drain(u, _):
        @pl.when(i == 0)
        def _():
            part = slot.at[u, :, pl.ds(0, 7)]
            pltpu.make_async_copy(part, part, init_ss.at[u]).wait()

        @pl.when(i == 1)
        def _():
            part = slot.at[u, :, pl.ds(0, 8)]
            pltpu.make_async_copy(part, part, init_ss.at[u]).wait()

        @pl.when(i < 7)
        def _():
            pltpu.make_async_copy(slot.at[u], slot.at[u], next_ss.at[u]).wait()
        sibling(u, 0).wait_send()

        @pl.when(d == 0)
        def _():
            sibling(u, 1).wait_send()
            partial(u).wait_send()
        three = obuf.at[u, pl.ds(0, 3)]
        pltpu.make_async_copy(three, three, out_ss.at[u]).wait()
        pltpu.make_async_copy(obuf.at[u, 0], obuf.at[u, 0], out_ls.at[u]).wait()
        return 0

    lax.fori_loop(0, UP_VALUES, drain, 0)
    pltpu.make_async_copy(out.at[pl.ds(0, 12)], out.at[pl.ds(0, 12)], out_rs).wait()


def on_device(env_in, mps, proj, mpo, mpo_charge, block_sizes):
    bf16 = jnp.bfloat16
    vm = pl.BlockSpec(memory_space=pltpu.VMEM)
    sm = pl.BlockSpec(memory_space=pltpu.SMEM)
    hbm = pl.BlockSpec(memory_space=pl.ANY)
    dma = pltpu.SemaphoreType.DMA
    out = pl.pallas_call(
        kernel,
        out_shape=jax.ShapeDtypeStruct((SECTORS, BLOCK, BLOCK), bf16),
        in_specs=[sm, sm, vm, hbm, hbm, hbm],
        out_specs=hbm,
        scratch_shapes=[
            pltpu.VMEM((UP_VALUES, 2, 16, 16, 256), bf16),
            pltpu.VMEM((2, 1024, 256), bf16),
            pltpu.VMEM((1024, 256), bf16),
            pltpu.VMEM((2, 4, HALF, BLOCK), jnp.float32),
            pltpu.VMEM((UP_VALUES, 2, 4, HALF, BLOCK), bf16),
            pltpu.VMEM((UP_VALUES, 2, 4, HALF, BLOCK), bf16),
            pltpu.VMEM((UP_VALUES, 4, HALF, BLOCK), bf16),
            pltpu.VMEM((UP_VALUES, 4, HALF, BLOCK), bf16),
            pltpu.VMEM((UP_VALUES, 2, 4, 16, 256), bf16),
            pltpu.VMEM((UP_VALUES, 4, HALF, BLOCK), bf16),
            pltpu.VMEM((2, UP_VALUES, 2, 16, 256), bf16),
            pltpu.VMEM((UP_VALUES, 2, 2, BLOCK, BLOCK), bf16),
            pltpu.VMEM((UP_VALUES + 1, 2, 4, HALF, BLOCK), bf16),
            dma((8,)), dma((8,)), dma((8,)), dma((8, 2)), dma((8, 2)), dma((8,)), dma((8,)), dma((8,)), dma((8,)),
            dma((9,)), dma,
        ],
        compiler_params=pltpu.CompilerParams(collective_id=0, has_side_effects=True, vmem_limit_bytes=40 << 20),
        name="sweep",
    )(
        mpo_charge, block_sizes, mpo.reshape(64, 64),
        env_in.reshape(UP_VALUES, 2, 2, 2, 2, 16, BLOCK),
        mps.reshape(4, UP_VALUES, DOWN_VALUES, BLOCK, BLOCK),
        proj.reshape(4, UP_VALUES, DOWN_VALUES, BLOCK, BLOCK),
    )
    return out[None, None]


def solution(mesh):
    return jax.shard_map(
        on_device,
        mesh=mesh,
        in_specs=(
            P("op", None, None, None),
            P("chain", None, None, None, None),
            P("chain", None, None, None, None),
            P("chain", None, None, None, None),
            P(),
            P(),
        ),
        out_specs=P("chain", "op", None, None, None),
        check_vma=False,
    )
```

time: 249 us -> 150 us (0.60)
  Pallas kernels: 212 us -> 141 us
  local copies, waits for them, and re-layouts: 30.5 us -> 8.02 us
  other arithmetic: 5.94 us -> 0 us
    pallas_call x1, Pallas kernels: 212 us -> 141 us  [on_device(): pl.pallas_call(kernel, out_shape=jax.ShapeDtypeStruct((SECTORS, BLOCK, BL...]
    rev x1 -> x0, local copies, waits for them, and re-layouts: 15.2 us -> none  [on_device(): stacked = jnp.where(k == 0, stacked, stacked[:, :, :, :, ::-1])]
    unnamed x16 -> x11, local copies, waits for them, and re-layouts: 2.63 us -> 7.77 us
    transpose x1 -> x0, other arithmetic: 3.75 us -> none  [on_device(): proj_cols = stacked.transpose(0, 4, 5, 2, 1, 3).reshape(SECTORS, BLOCK, 256)]
    squeeze x2 -> x0, local copies, waits for them, and re-layouts: 2.97 us -> none  [the longest x1 1.89 us: on_device(): part = pgrid[t][:UP_VALUES - up, :DOWN_VALUES - down]]
where the time goes in v2:
time: 150 us; the launch traced here: 149 us
  Pallas kernels  141 us (94%)
  local copies, waits for them, and re-layouts  8.02 us (5%)
    pallas_call x1, Pallas kernels, on_device(): pl.pallas_call(kernel, out_shape=jax.ShapeDtypeStruct((SECTORS, BLOCK, BL...  141 us
    unnamed x11, local copies, waits for them, and re-layouts  7.77 us

profile of v2, /device:TPU:39, one launch (start us, length us, event | category | flops | bytes accessed | tf_op | source)
XLA Modules:
  0.0 149.4 jit_solution(1224293057990127872)
XLA Ops:
  0.0 0.8 copy.10.charge
  0.8 1.3 copy.9
  2.1 0.2 reshape.12.coeff
  2.3 0.0 copy-start
  2.3 1.6 %copy-done = bf16[1,4,16,128,128]{4,3,2,1,0:T(8,128)(2,1)S(1)} copy-done((bf16[1,4,16,128,128]{4,3,2,1,0:T(8,128)(2,1)S(1)}, bf16[1,4,16,128,128]{4,3,2,1,0:T(8,128)(2,1)}, u32[]{:S(2)}) %copy-start) | copy-done | bytes 2097176
  3.9 0.0 copy-start.1
  3.9 1.6 %copy-done.1 = bf16[1,4,16,128,128]{4,3,2,1,0:T(8,128)(2,1)S(1)} copy-done((bf16[1,4,16,128,128]{4,3,2,1,0:T(8,128)(2,1)S(1)}, bf16[1,4,16,128,128]{4,3,2,1,0:T(8,128)(2,1)}, u32[]{:S(2)}) %copy-start.1) | copy-done | bytes 2097176
  5.5 0.0 copy-start.2
  5.5 1.0 copy-done.2
  6.5 0.0 copy-start.3
  6.5 0.7 copy-done.3
  7.2 141.4 %sweep.1 = bf16[16,128,128]{2,1,0:T(8,128)(2,1)S(1)} custom-call(s32[16,2]{1,0:T(8,128)S(1)} %copy.10.charge, s32[9,16]{1,0:T(8,128)S(1)} %copy-done.3, bf16[64,64]{1,0:T(8,128)(2,1)S(1)} %reshape.12.coeff, bf16[8,2,2,2,2,16,128]{6,5,4,3,2,1,0:T(8,128)(2,1)S(1)} %bitcast.9, bf16[4,8,2,128,128]{4,3,2,1,0:T(8,128)(2,1)S(1)} %bitcast.7, ...), custom_call_target="tpu_custom_call" | custom-call | tf_op jit(solution)/shard_map/sweep/pallas_call | solution.py:338
  148.6 0.8 copy.12
Async XLA Ops:
  2.3 1.6 %copy-start = (bf16[1,4,16,128,128]{4,3,2,1,0:T(8,128)(2,1)S(1)}, bf16[1,4,16,128,128]{4,3,2,1,0:T(8,128)(2,1)}, u32[]{:S(2)}) copy-start(bf16[1,4,16,128,128]{4,3,2,1,0:T(8,128)(2,1)} %param.7) | copy-start | bytes 6291460
  3.9 1.6 %copy-start.1 = (bf16[1,4,16,128,128]{4,3,2,1,0:T(8,128)(2,1)S(1)}, bf16[1,4,16,128,128]{4,3,2,1,0:T(8,128)(2,1)}, u32[]{:S(2)}) copy-start(bf16[1,4,16,128,128]{4,3,2,1,0:T(8,128)(2,1)} %param.8) | copy-start | bytes 6291460
  5.5 1.0 copy-start.2
  6.5 0.7 copy-start.3

commit v3 on v2

--- a/solution.py
+++ b/solution.py
@@ -10,12 +10,12 @@
 SECTORS = 16
 BLOCK = 128
 HALF = 64
-AHEAD = 3
 MESH = pl.DeviceIdType.MESH
 
 UP_CHARGE = (0, 1, 0, 1)
 DOWN_CHARGE = (0, 0, 1, 1)
 PHYS_ORDER = (0, 2, 1, 3)
+INIT_ROUTES = ((0, 0, (0, 1)), (1, 1, (0, 3)), (2, 0, (2, 3)), (7, 1, (1, 2)))
 
 
 def role_of(op):
@@ -42,6 +42,11 @@
 
     bar = pltpu.get_barrier_semaphore()
 
+    def near(step, flip, half):
+        z = (op // 2) % 2
+        z = 1 - z if flip else z
+        return (op // 4 + step) % 4 * 4 + z * 2 + half
+
     def greet(chain, group, down, half):
         pl.semaphore_signal(bar, inc=1, device_id=(chain, op_of(group, down, half)), device_id_type=MESH)
 
@@ -52,25 +57,26 @@
 
     @pl.when(i == 0)
     def _():
-        for j in range(8):
-            greet(1, (g + j // 2) % 4, 1 - d, (k + j) % 2)
-        for j in range(2, 8):
-            greet(0, (g + j // 2) % 4, d, (k + j) % 2)
+        for source, flip, steps in INIT_ROUTES:
+            for step in steps:
+                for half in range(2):
+                    if source or step:
+                        pl.semaphore_signal(
+                            bar, inc=1, device_id=(source, near(4 - step, flip, half)), device_id_type=MESH)
     greet(i, g, d, 1 - k)
     greet(i, g, 1 - d, k)
     greet(i, g, 1 - d, 1 - k)
 
-    target_down = (d + i) % 2
-
-    def env_load(half, side):
-        return pltpu.make_async_copy(
-            env.at[:, target_down, half, :, side], env_r.at[half, :, :, :, pl.ds(side * BLOCK, BLOCK)], load_sem.at[0])
-
-    @pl.when(i < 2)
-    def _():
-        for half in range(2):
-            for side in range(2):
-                env_load(half, side).start()
+    spreads = (i < 3) | (i == 7)
+
+    @pl.when(spreads)
+    def _():
+        for down in range(2):
+            for half in range(2):
+                for side in range(2):
+                    pltpu.make_async_copy(
+                        env.at[:, down, half, :, side], env_r.at[down, half, :, :, :, pl.ds(side * BLOCK, BLOCK)],
+                        load_sem.at[0]).start()
 
     def mps_load(p):
         up = UP_CHARGE[p]
@@ -134,50 +140,43 @@
 
     @pl.when(i == 0)
     def _():
-        pl.semaphore_wait(bar, 13)
-
-    @pl.when(i == 1)
-    def _():
-        pl.semaphore_wait(bar, 15)
-
-    @pl.when((i > 1) & (i < 7))
+        pl.semaphore_wait(bar, 9)
+
+    @pl.when((i == 1) | (i == 2))
+    def _():
+        pl.semaphore_wait(bar, 11)
+
+    @pl.when(i > 2)
     def _():
         pl.semaphore_wait(bar, 7)
 
-    @pl.when(i == 7)
-    def _():
-        pl.semaphore_wait(bar, 3)
-
     place = g * 4 + me
 
-    def init_row(u, first):
-        for j in range(first, 8):
-            half = (k + j) % 2
-            pltpu.make_async_remote_copy(
-                env_r.at[half, u], slot.at[u, :, place], init_ss.at[u], slot_sem.at[u],
-                device_id=(0, op_of((g + j // 2) % 4, target_down, half)), device_id_type=MESH).start()
-
-    def init_own(u):
-        init_row(u, 1)
-        pltpu.make_async_copy(env_r.at[k, u], slot.at[u, :, place], slot_sem.at[u]).start()
-
-    @pl.when(i < 2)
+    @pl.when(spreads)
     def _():
         pltpu.make_async_copy(env_r, env_r, load_sem.at[0]).wait()
 
-    @pl.when(i == 0)
-    def _():
-        def start(u, _):
-            init_own(u)
+    for source, flip, steps in INIT_ROUTES:
+        def init_row(u, _):
+            for step in steps:
+                down = (op // 4 + step) % 4 // 2
+                for half in range(2):
+                    copy = pltpu.make_async_remote_copy(
+                        env_r.at[down, half, u], slot.at[u, :, place], init_ss.at[u], slot_sem.at[u],
+                        device_id=(0, near(step, flip, half)), device_id_type=MESH)
+                    if source or step:
+                        copy.start()
+                    else:
+                        @pl.when(half != k)
+                        def _():
+                            copy.start()
+            if source == 0:
+                pltpu.make_async_copy(env_r.at[d, k, u], slot.at[u, :, place], slot_sem.at[u]).start()
             return 0
-        lax.fori_loop(0, AHEAD, start, 0)
-
-    @pl.when(i == 1)
-    def _():
-        def start(u, _):
-            init_row(u, 0)
-            return 0
-        lax.fori_loop(0, UP_VALUES, start, 0)
+
+        @pl.when(i == source)
+        def _():
+            lax.fori_loop(0, UP_VALUES, init_row, 0)
 
     for p in range(4):
         mps_load(p).wait()
@@ -231,10 +230,17 @@
             part_s.at[u], part_r.at[u], part_ss.at[u], part_rs.at[u],
             device_id=(i, op_of(g, 1 - d, k)), device_id_type=MESH)
 
+    def give(u, _):
+        dst = out.at[u * 2 + d, pl.ds(k * HALF, HALF)]
+        for j in range(1, 4):
+            m = (me + j) % 4
+            pltpu.make_async_remote_copy(
+                obuf.at[u, m], dst, out_ss.at[u], out_rs,
+                device_id=(i, bond_of(g, m)), device_id_type=MESH).start()
+        pltpu.make_async_copy(obuf.at[u, me], dst, out_ls.at[u]).start()
+        return 0
+
     def step(u, _):
-        @pl.when((i == 0) & (u < UP_VALUES - AHEAD))
-        def _():
-            init_own(u + AHEAD)
         pltpu.make_async_copy(slot.at[u], slot.at[u], slot_sem.at[u]).wait()
 
         @pl.when(d == 0)
@@ -251,6 +257,7 @@
         def _():
             apply(u, 1)
             sibling(u, 1).start()
+            mix(u, 1, 2)
 
         @pl.when(d == 1)
         def _():
@@ -285,30 +292,26 @@
                 part_s[u, m] = (own[1, m] + sib_r[u, 1, m].astype(f32)).astype(bf16)
             partial(u).start()
 
-        dst = out.at[u * 2 + d, pl.ds(k * HALF, HALF)]
-        for j in range(1, 4):
-            m = (me + j) % 4
-            pltpu.make_async_remote_copy(
-                obuf.at[u, m], dst, out_ss.at[u], out_rs,
-                device_id=(i, bond_of(g, m)), device_id_type=MESH).start()
-        pltpu.make_async_copy(obuf.at[u, me], dst, out_ls.at[u]).start()
-
-        @pl.when(d == 0)
-        def _():
-            mix(u, 1, 2)
+        @pl.when(i == 7)
+        def _():
+            give(u, 0)
         return 0
 
     lax.fori_loop(0, UP_VALUES, step, 0)
+
+    @pl.when(i < 7)
+    def _():
+        lax.fori_loop(0, UP_VALUES, give, 0)
 
     def drain(u, _):
         @pl.when(i == 0)
         def _():
-            part = slot.at[u, :, pl.ds(0, 7)]
+            part = slot.at[u, :, pl.ds(0, 3)]
             pltpu.make_async_copy(part, part, init_ss.at[u]).wait()
 
-        @pl.when(i == 1)
-        def _():
-            part = slot.at[u, :, pl.ds(0, 8)]
+        @pl.when(spreads & (i > 0))
+        def _():
+            part = slot.at[u, :, pl.ds(0, 4)]
             pltpu.make_async_copy(part, part, init_ss.at[u]).wait()
 
         @pl.when(i < 7)
@@ -333,7 +336,7 @@
     bf16 = jnp.bfloat16
     vm = pl.BlockSpec(memory_space=pltpu.VMEM)
     sm = pl.BlockSpec(memory_space=pltpu.SMEM)
-    hbm = pl.BlockSpec(memory_space=pl.ANY)
+    hbm = pl.BlockSpec(memory_space=pltpu.HBM)
     dma = pltpu.SemaphoreType.DMA
     out = pl.pallas_call(
         kernel,
@@ -351,13 +354,13 @@
             pltpu.VMEM((UP_VALUES, 4, HALF, BLOCK), bf16),
             pltpu.VMEM((UP_VALUES, 2, 4, 16, 256), bf16),
             pltpu.VMEM((UP_VALUES, 4, HALF, BLOCK), bf16),
-            pltpu.VMEM((2, UP_VALUES, 2, 16, 256), bf16),
+            pltpu.VMEM((2, 2, UP_VALUES, 2, 16, 256), bf16),
             pltpu.VMEM((UP_VALUES, 2, 2, BLOCK, BLOCK), bf16),
             pltpu.VMEM((UP_VALUES + 1, 2, 4, HALF, BLOCK), bf16),
             dma((8,)), dma((8,)), dma((8,)), dma((8, 2)), dma((8, 2)), dma((8,)), dma((8,)), dma((8,)), dma((8,)),
             dma((9,)), dma,
         ],
-        compiler_params=pltpu.CompilerParams(collective_id=0, has_side_effects=True, vmem_limit_bytes=40 << 20),
+        compiler_params=pltpu.CompilerParams(collective_id=0, has_side_effects=True, vmem_limit_bytes=56 << 20),
         name="sweep",
     )(
         mpo_charge, block_sizes, mpo.reshape(64, 64),

time: 150 us -> 150 us (level)
  Pallas kernels: 141 us -> 144 us
  local copies, waits for them, and re-layouts: 8.02 us -> 5.39 us
    unnamed x11 -> x3, local copies, waits for them, and re-layouts: 7.77 us -> 4.54 us
    pallas_call x1, Pallas kernels: 141 us -> 144 us  [on_device(): pl.pallas_call(kernel, out_shape=jax.ShapeDtypeStruct((SECTORS, BLOCK, BL...]
where the time goes in v3:
time: 150 us
  Pallas kernels  144 us (96%)
  local copies, waits for them, and re-layouts  5.39 us (4%)
    pallas_call x1, Pallas kernels, on_device(): pl.pallas_call(kernel, out_shape=jax.ShapeDtypeStruct((SECTORS, BLOCK, BL...  144 us
    unnamed x3, local copies, waits for them, and re-layouts  4.54 us

profile of v3, /device:TPU:39, one launch (start us, length us, event | category | flops | bytes accessed | tf_op | source)
XLA Modules:
  0.0 149.9 jit_solution(14408191336086172464)
XLA Ops:
  0.0 1.3 copy.10.charge
  1.3 1.3 copy.9
  2.7 0.9 reshape.12.coeff
  3.5 144.5 %sweep.1 = bf16[16,128,128]{2,1,0:T(8,128)(2,1)} custom-call(s32[16,2]{1,0:T(8,128)} %copy.10.charge, s32[9,16]{1,0:T(8,128)} %sizes.1, bf16[64,64]{1,0:T(8,128)(2,1)} %reshape.12.coeff, bf16[8,2,2,2,2,16,128]{6,5,4,3,2,1,0:T(8,128)(2,1)} %bitcast.9, bf16[4,8,2,128,128]{4,3,2,1,0:T(8,128)(2,1)} %bitcast.7, bf16[4,8,2,128,128]{4,3,2,1,0:T(8,128)(2,1)} %bitcast.8), custom_call_target="tpu_custom_call" | custom-call | tf_op jit(solution)/shard_map/sweep/pallas_call | solution.py:341
  148.0 1.9 %copy.12 = bf16[1,1,16,128,128]{4,3,2,1,0:T(8,128)(2,1)} copy(bf16[1,1,16,128,128]{4,3,2,1,0:T(8,128)(2,1)} %bitcast.6) | data formatting | bytes 1048576

commit v4 on v3

--- a/solution.py
+++ b/solution.py
@@ -15,7 +15,7 @@
 UP_CHARGE = (0, 1, 0, 1)
 DOWN_CHARGE = (0, 0, 1, 1)
 PHYS_ORDER = (0, 2, 1, 3)
-INIT_ROUTES = ((0, 0, (0, 1)), (1, 1, (0, 3)), (2, 0, (2, 3)), (7, 1, (1, 2)))
+INIT_ROUTES = ((0, 0, (0,)), (2, 0, (1, 3)), (6, 0, (2,)), (3, 1, (0, 3)), (7, 1, (1, 2)))
 
 
 def role_of(op):
@@ -67,7 +67,7 @@
     greet(i, g, 1 - d, k)
     greet(i, g, 1 - d, 1 - k)
 
-    spreads = (i < 3) | (i == 7)
+    spreads = (i == 0) | (i == 2) | (i == 3) | (i > 5)
 
     @pl.when(spreads)
     def _():
@@ -138,15 +138,15 @@
         tall = jnp.dot(repeat, wide, preferred_element_type=f32)
         mb[place * 256:(place + 1) * 256, :] = jnp.where(long_rows % 16 == long_cols % 16, tall, 0.0).astype(bf16)
 
-    @pl.when(i == 0)
+    @pl.when((i == 2) | (i == 3))
+    def _():
+        pl.semaphore_wait(bar, 11)
+
+    @pl.when(i == 6)
     def _():
         pl.semaphore_wait(bar, 9)
 
-    @pl.when((i == 1) | (i == 2))
-    def _():
-        pl.semaphore_wait(bar, 11)
-
-    @pl.when(i > 2)
+    @pl.when((i < 2) | (i == 4) | (i == 5) | (i == 7))
     def _():
         pl.semaphore_wait(bar, 7)
 
@@ -155,9 +155,17 @@
     @pl.when(spreads)
     def _():
         pltpu.make_async_copy(env_r, env_r, load_sem.at[0]).wait()
+
+    def init_sent(u, count):
+        part = slot.at[u, :, pl.ds(0, count)]
+        pltpu.make_async_copy(part, part, init_ss.at[u]).wait()
 
     for source, flip, steps in INIT_ROUTES:
         def init_row(u, _):
+            if source:
+                @pl.when(u >= 2)
+                def _():
+                    init_sent(u - 2, 2 * len(steps))
             for step in steps:
                 down = (op // 4 + step) % 4 // 2
                 for half in range(2):
@@ -177,6 +185,9 @@
         @pl.when(i == source)
         def _():
             lax.fori_loop(0, UP_VALUES, init_row, 0)
+            if source:
+                init_sent(UP_VALUES - 2, 2 * len(steps))
+                init_sent(UP_VALUES - 1, 2 * len(steps))
 
     for p in range(4):
         mps_load(p).wait()
@@ -306,13 +317,7 @@
     def drain(u, _):
         @pl.when(i == 0)
         def _():
-            part = slot.at[u, :, pl.ds(0, 3)]
-            pltpu.make_async_copy(part, part, init_ss.at[u]).wait()
-
-        @pl.when(spreads & (i > 0))
-        def _():
-            part = slot.at[u, :, pl.ds(0, 4)]
-            pltpu.make_async_copy(part, part, init_ss.at[u]).wait()
+            init_sent(u, 1)
 
         @pl.when(i < 7)
         def _():

time: 150 us -> 139 us (0.927)
  Pallas kernels: 144 us -> 134 us
    pallas_call x1, Pallas kernels: 144 us -> 134 us  [on_device(): pl.pallas_call(kernel, out_shape=jax.ShapeDtypeStruct((SECTORS, BLOCK, BL...]
where the time goes in v4:
time: 139 us
  Pallas kernels  134 us (96%)
  local copies, waits for them, and re-layouts  5.39 us (4%)
    pallas_call x1, Pallas kernels, on_device(): pl.pallas_call(kernel, out_shape=jax.ShapeDtypeStruct((SECTORS, BLOCK, BL...  134 us
    unnamed x3, local copies, waits for them, and re-layouts  4.54 us

profile of v4, /device:TPU:39, one launch (start us, length us, event | category | flops | bytes accessed | tf_op | source)
XLA Modules:
  0.0 139.0 jit_solution(17293769676686703842)
XLA Ops:
  0.0 1.3 copy.10.charge
  1.3 1.3 copy.9
  2.7 0.9 reshape.12.coeff
  3.5 133.6 %sweep.1 = bf16[16,128,128]{2,1,0:T(8,128)(2,1)} custom-call(s32[16,2]{1,0:T(8,128)} %copy.10.charge, s32[9,16]{1,0:T(8,128)} %sizes.1, bf16[64,64]{1,0:T(8,128)(2,1)} %reshape.12.coeff, bf16[8,2,2,2,2,16,128]{6,5,4,3,2,1,0:T(8,128)(2,1)} %bitcast.9, bf16[4,8,2,128,128]{4,3,2,1,0:T(8,128)(2,1)} %bitcast.7, bf16[4,8,2,128,128]{4,3,2,1,0:T(8,128)(2,1)} %bitcast.8), custom_call_target="tpu_custom_call" | custom-call | tf_op jit(solution)/shard_map/sweep/pallas_call | solution.py:346
  137.1 1.9 %copy.12 = bf16[1,1,16,128,128]{4,3,2,1,0:T(8,128)(2,1)} copy(bf16[1,1,16,128,128]{4,3,2,1,0:T(8,128)(2,1)} %bitcast.6) | data formatting | bytes 1048576

commit v5 on v4

--- a/solution.py
+++ b/solution.py
@@ -91,6 +91,54 @@
     for p in range(4):
         mps_load(p).start()
         proj_load(p).start()
+    for count, sites in ((7, (0, 1, 4, 5, 7)), (11, (2, 3)), (9, (6,))):
+        here = i == sites[0]
+        for other in sites[1:]:
+            here = here | (i == other)
+
+        @pl.when(here)
+        def _():
+            pl.semaphore_wait(bar, count)
+
+    place = g * 4 + me
+
+    @pl.when(spreads)
+    def _():
+        pltpu.make_async_copy(env_r, env_r, load_sem.at[0]).wait()
+
+    def init_sent(u, count):
+        part = slot.at[u, :, pl.ds(0, count)]
+        pltpu.make_async_copy(part, part, init_ss.at[u]).wait()
+
+    def spread(first, last):
+        for source, flip, steps in INIT_ROUTES:
+            def init_row(u, _):
+                if source and first:
+                    init_sent(u - 2, 2 * len(steps))
+                for step in steps:
+                    down = (op // 4 + step) % 4 // 2
+                    for half in range(2):
+                        copy = pltpu.make_async_remote_copy(
+                            env_r.at[down, half, u], slot.at[u, :, place], init_ss.at[u], slot_sem.at[u],
+                            device_id=(0, near(step, flip, half)), device_id_type=MESH)
+                        if source or step:
+                            copy.start()
+                        else:
+                            @pl.when(half != k)
+                            def _():
+                                copy.start()
+                if source == 0:
+                    pltpu.make_async_copy(env_r.at[d, k, u], slot.at[u, :, place], slot_sem.at[u]).start()
+                return 0
+
+            @pl.when(i == source)
+            def _():
+                lax.fori_loop(first, last, init_row, 0)
+                if source and first:
+                    init_sent(UP_VALUES - 2, 2 * len(steps))
+                    init_sent(UP_VALUES - 1, 2 * len(steps))
+
+    spread(0, 2)
     zero = jnp.zeros((HALF, BLOCK), bf16)
     for t in range(4):
         pcols[UP_VALUES, 0, t] = zero
@@ -102,7 +150,7 @@
                 pcols[up, 0, t] = zero
     for plane in range(2):
         mrows[0, plane, 1] = jnp.zeros((BLOCK, BLOCK), bf16)
-    lbuf[...] = jnp.zeros_like(lbuf)
+    lbuf[2] = jnp.zeros((2, 1024, BLOCK), bf16)
 
     rows = lax.broadcasted_iota(jnp.int32, (16, 64), 0)
     cols = lax.broadcasted_iota(jnp.int32, (16, 64), 1)
@@ -130,64 +178,13 @@
     repeat = jnp.where(
         lax.broadcasted_iota(jnp.int32, (256, 16), 0) // 16 == lax.broadcasted_iota(jnp.int32, (256, 16), 1),
         1.0, 0.0).astype(bf16)
-    for place, p in enumerate(PHYS_ORDER):
+    for rank, p in enumerate(PHYS_ORDER):
         widen = jnp.where(rows == slot_bond * 4 + p, 1.0, 0.0).astype(bf16)
         wide = jnp.dot(mine, widen, preferred_element_type=f32)
         match = (col_up == row_up + UP_CHARGE[p]) & (col_down == row_down + DOWN_CHARGE[p])
         wide = jnp.where(match, wide, 0.0).astype(bf16)
         tall = jnp.dot(repeat, wide, preferred_element_type=f32)
-        mb[place * 256:(place + 1) * 256, :] = jnp.where(long_rows % 16 == long_cols % 16, tall, 0.0).astype(bf16)
-
-    @pl.when((i == 2) | (i == 3))
-    def _():
-        pl.semaphore_wait(bar, 11)
-
-    @pl.when(i == 6)
-    def _():
-        pl.semaphore_wait(bar, 9)
-
-    @pl.when((i < 2) | (i == 4) | (i == 5) | (i == 7))
-    def _():
-        pl.semaphore_wait(bar, 7)
-
-    place = g * 4 + me
-
-    @pl.when(spreads)
-    def _():
-        pltpu.make_async_copy(env_r, env_r, load_sem.at[0]).wait()
-
-    def init_sent(u, count):
-        part = slot.at[u, :, pl.ds(0, count)]
-        pltpu.make_async_copy(part, part, init_ss.at[u]).wait()
-
-    for source, flip, steps in INIT_ROUTES:
-        def init_row(u, _):
-            if source:
-                @pl.when(u >= 2)
-                def _():
-                    init_sent(u - 2, 2 * len(steps))
-            for step in steps:
-                down = (op // 4 + step) % 4 // 2
-                for half in range(2):
-                    copy = pltpu.make_async_remote_copy(
-                        env_r.at[down, half, u], slot.at[u, :, place], init_ss.at[u], slot_sem.at[u],
-                        device_id=(0, near(step, flip, half)), device_id_type=MESH)
-                    if source or step:
-                        copy.start()
-                    else:
-                        @pl.when(half != k)
-                        def _():
-                            copy.start()
-            if source == 0:
-                pltpu.make_async_copy(env_r.at[d, k, u], slot.at[u, :, place], slot_sem.at[u]).start()
-            return 0
-
-        @pl.when(i == source)
-        def _():
-            lax.fori_loop(0, UP_VALUES, init_row, 0)
-            if source:
-                init_sent(UP_VALUES - 2, 2 * len(steps))
-                init_sent(UP_VALUES - 1, 2 * len(steps))
+        mb[rank * 256:(rank + 1) * 256, :] = jnp.where(long_rows % 16 == long_cols % 16, tall, 0.0).astype(bf16)
 
     for p in range(4):
         mps_load(p).wait()
@@ -205,18 +202,21 @@
     lax.fori_loop(0, UP_VALUES, mask_row, 0)
     for t in range(4):
         proj_load(t).wait()
-
-    def mix(u, first, planes):
+    spread(2, UP_VALUES)
+
+    def mix(u, first):
+        place = first * (1 + u % 2)
         for pair in range(2):
             x = slot[u, pair].reshape(256, 256)
-            y = jnp.dot(mb[first * 512:first * 512 + planes * 256, :], x, preferred_element_type=f32).astype(bf16)
+            y = jnp.dot(mb[pl.ds(pl.multiple_of(first * 512, 512), 512), :], x, preferred_element_type=f32).astype(bf16)
             for side in range(2):
-                for plane in range(planes):
-                    lbuf[plane, pl.ds((2 * pair + side) * 256, 256), pl.ds(first * BLOCK, BLOCK)] = (
+                for plane in range(2):
+                    lbuf[place, plane, pl.ds((2 * pair + side) * 256, 256)] = (
                         y[plane * 256:(plane + 1) * 256, side * BLOCK:(side + 1) * BLOCK])
 
     def apply(u, plane):
-        grown = jnp.dot(lbuf[plane], mrows[u, plane].reshape(256, BLOCK), preferred_element_type=f32).astype(bf16)
+        both = jnp.concatenate([lbuf[0, plane], lbuf[1 + (u + 1) % 2, plane]], axis=1)
+        grown = jnp.dot(both, mrows[u, plane].reshape(256, BLOCK), preferred_element_type=f32).astype(bf16)
         for m in range(4):
             b = bond_of(g, m)
             up = u + charge[b, 0]
@@ -241,38 +241,18 @@
             part_s.at[u], part_r.at[u], part_ss.at[u], part_rs.at[u],
             device_id=(i, op_of(g, 1 - d, k)), device_id_type=MESH)
 
-    def give(u, _):
-        dst = out.at[u * 2 + d, pl.ds(k * HALF, HALF)]
-        for j in range(1, 4):
-            m = (me + j) % 4
-            pltpu.make_async_remote_copy(
-                obuf.at[u, m], dst, out_ss.at[u], out_rs,
-                device_id=(i, bond_of(g, m)), device_id_type=MESH).start()
-        pltpu.make_async_copy(obuf.at[u, me], dst, out_ls.at[u]).start()
-        return 0
-
-    def step(u, _):
-        pltpu.make_async_copy(slot.at[u], slot.at[u], slot_sem.at[u]).wait()
-
-        @pl.when(d == 0)
-        def _():
-            mix(u, 0, 2)
-
-        @pl.when(d == 1)
-        def _():
-            mix(u, 0, 1)
-        apply(u, 0)
-        sibling(u, 0).start()
-
-        @pl.when(d == 0)
-        def _():
-            apply(u, 1)
-            sibling(u, 1).start()
-            mix(u, 1, 2)
-
-        @pl.when(d == 1)
-        def _():
-            mix(u, 1, 1)
+    def to_next(u, group):
+        return pltpu.make_async_remote_copy(
+            sbuf.at[u], slot.at[u, :, pl.ds(g * 4, 4)], next_ss.at[u], slot_sem.at[u],
+            device_id=(i + 1, op_of(group, d, k)), device_id_type=MESH)
+
+    def hand_over(u):
+        sibling(u, 1).wait_recv()
+        for m in range(4):
+            part_s[u, m] = (own[1, m] + sib_r[u, 1, m].astype(f32)).astype(bf16)
+        partial(u).start()
+
+    def finish(u):
         sibling(u, 0).wait_recv()
 
         @pl.when(d == 1)
@@ -283,7 +263,7 @@
 
         for m in range(4):
             res = (own[0, m] + sib_r[u, 0, m].astype(f32)).astype(bf16)
-            obuf[u, m] = res
+            obuf[m, u] = res
             for pair in range(2):
                 for side in range(2):
                     start = pair * 32 + side * 16
@@ -292,27 +272,54 @@
         @pl.when(i < 7)
         def _():
             for j in range(4):
+                to_next(u, (g + j) % 4).start()
+
+        @pl.when(i > 5)
+        def _():
+            for j in range(1, 4):
+                m = (me + j) % 4
                 pltpu.make_async_remote_copy(
-                    sbuf.at[u], slot.at[u, :, pl.ds(g * 4, 4)], next_ss.at[u], slot_sem.at[u],
-                    device_id=(i + 1, op_of((g + j) % 4, d, k)), device_id_type=MESH).start()
-
-        @pl.when(d == 0)
-        def _():
-            sibling(u, 1).wait_recv()
-            for m in range(4):
-                part_s[u, m] = (own[1, m] + sib_r[u, 1, m].astype(f32)).astype(bf16)
-            partial(u).start()
-
-        @pl.when(i == 7)
-        def _():
-            give(u, 0)
+                    obuf.at[m, u], out.at[u, d, k], out_ss.at[u], out_rs,
+                    device_id=(i, bond_of(g, m)), device_id_type=MESH).start()
+            pltpu.make_async_copy(obuf.at[me, u], out.at[u, d, k], out_ls.at[u]).start()
+
+    def step(n, _):
+        u, plane = n // 2, n % 2
+
+        @pl.when(plane == 0)
+        def _():
+            pltpu.make_async_copy(slot.at[u], slot.at[u], slot_sem.at[u]).wait()
+
+        @pl.when(n < 2 * UP_VALUES - 1)
+        def _():
+            mix(u, plane)
+
+        @pl.when((plane == 0) | (d == 0))
+        def _():
+            apply(u, plane)
+            sibling(u, plane).start()
+
+        @pl.when(plane == 0)
+        def _():
+            finish(u)
+
+        @pl.when((plane == 1) & (d == 0))
+        def _():
+            hand_over(u)
         return 0
 
-    lax.fori_loop(0, UP_VALUES, step, 0)
-
-    @pl.when(i < 7)
+    lax.fori_loop(0, 2 * UP_VALUES, step, 0)
+
+    @pl.when(i < 6)
     def _():
-        lax.fori_loop(0, UP_VALUES, give, 0)
+        for j in range(1, 4):
+            m = (me + j) % 4
+            pltpu.make_async_remote_copy(
+                obuf.at[m], out.at[:, d, k], out_ss.at[0], out_rs,
+                device_id=(i, bond_of(g, m)), device_id_type=MESH).start()
+        pltpu.make_async_copy(obuf.at[me], out.at[:, d, k], out_ls.at[0]).start()
+        pltpu.make_async_copy(obuf.at[pl.ds(0, 3)], obuf.at[pl.ds(0, 3)], out_ss.at[0]).wait()
+        pltpu.make_async_copy(obuf.at[0], obuf.at[0], out_ls.at[0]).wait()
 
     def drain(u, _):
         @pl.when(i == 0)
@@ -328,13 +335,16 @@
         def _():
             sibling(u, 1).wait_send()
             partial(u).wait_send()
-        three = obuf.at[u, pl.ds(0, 3)]
-        pltpu.make_async_copy(three, three, out_ss.at[u]).wait()
-        pltpu.make_async_copy(obuf.at[u, 0], obuf.at[u, 0], out_ls.at[u]).wait()
+
+        @pl.when(i > 5)
+        def _():
+            three = obuf.at[pl.ds(0, 3), u]
+            pltpu.make_async_copy(three, three, out_ss.at[u]).wait()
+            pltpu.make_async_copy(obuf.at[0, u], obuf.at[0, u], out_ls.at[u]).wait()
         return 0
 
     lax.fori_loop(0, UP_VALUES, drain, 0)
-    pltpu.make_async_copy(out.at[pl.ds(0, 12)], out.at[pl.ds(0, 12)], out_rs).wait()
+    pltpu.make_async_copy(out.at[pl.ds(0, 6)], out.at[pl.ds(0, 6)], out_rs).wait()
 
 
 def on_device(env_in, mps, proj, mpo, mpo_charge, block_sizes):
@@ -345,12 +355,12 @@
     dma = pltpu.SemaphoreType.DMA
     out = pl.pallas_call(
         kernel,
-        out_shape=jax.ShapeDtypeStruct((SECTORS, BLOCK, BLOCK), bf16),
+        out_shape=jax.ShapeDtypeStruct((UP_VALUES, DOWN_VALUES, 2, HALF, BLOCK), bf16),
         in_specs=[sm, sm, vm, hbm, hbm, hbm],
         out_specs=hbm,
         scratch_shapes=[
             pltpu.VMEM((UP_VALUES, 2, 16, 16, 256), bf16),
-            pltpu.VMEM((2, 1024, 256), bf16),
+            pltpu.VMEM((3, 2, 1024, BLOCK), bf16),
             pltpu.VMEM((1024, 256), bf16),
             pltpu.VMEM((2, 4, HALF, BLOCK), jnp.float32),
             pltpu.VMEM((UP_VALUES, 2, 4, HALF, BLOCK), bf16),
@@ -358,7 +368,7 @@
             pltpu.VMEM((UP_VALUES, 4, HALF, BLOCK), bf16),
             pltpu.VMEM((UP_VALUES, 4, HALF, BLOCK), bf16),
             pltpu.VMEM((UP_VALUES, 2, 4, 16, 256), bf16),
-            pltpu.VMEM((UP_VALUES, 4, HALF, BLOCK), bf16),
+            pltpu.VMEM((4, UP_VALUES, HALF, BLOCK), bf16),
             pltpu.VMEM((2, 2, UP_VALUES, 2, 16, 256), bf16),
             pltpu.VMEM((UP_VALUES, 2, 2, BLOCK, BLOCK), bf16),
             pltpu.VMEM((UP_VALUES + 1, 2, 4, HALF, BLOCK), bf16),
@@ -373,7 +383,7 @@
         mps.reshape(4, UP_VALUES, DOWN_VALUES, BLOCK, BLOCK),
         proj.reshape(4, UP_VALUES, DOWN_VALUES, BLOCK, BLOCK),
     )
-    return out[None, None]
+    return out.reshape(1, 1, SECTORS, BLOCK, BLOCK)
 
 
 def solution(mesh):

time: 139 us -> 139 us (level)
  no operation moved by 1% of the time
where the time goes in v5:
time: 139 us
  Pallas kernels  134 us (96%)
  local copies, waits for them, and re-layouts  5.39 us (4%)
    pallas_call x1, Pallas kernels, on_device(): pl.pallas_call(kernel, out_shape=jax.ShapeDtypeStruct((UP_VALUES, DOWN_VA...  134 us
    unnamed x3, local copies, waits for them, and re-layouts  4.54 us

profile of v5, /device:TPU:39, one launch (start us, length us, event | category | flops | bytes accessed | tf_op | source)
XLA Modules:
  0.0 138.9 jit_solution(6924830344773368381)
XLA Ops:
  0.0 1.3 copy.10.charge
  1.3 1.3 copy.9
  2.7 0.9 reshape.15.coeff
  3.5 133.5 %sweep.1 = bf16[8,2,2,64,128]{4,3,2,1,0:T(8,128)(2,1)} custom-call(s32[16,2]{1,0:T(8,128)} %copy.10.charge, s32[9,16]{1,0:T(8,128)} %sizes.1, bf16[64,64]{1,0:T(8,128)(2,1)} %reshape.15.coeff, bf16[8,2,2,2,2,16,128]{6,5,4,3,2,1,0:T(8,128)(2,1)} %bitcast.9, bf16[4,8,2,128,128]{4,3,2,1,0:T(8,128)(2,1)} %bitcast.7, bf16[4,8,2,128,128]{4,3,2,1,0:T(8,128)(2,1)} %bitcast.8), custom_call_target="tpu_custom_call" | custom-call | tf_op jit(solution)/shard_map/sweep/pallas_call | solution.py:356
  137.0 1.9 %copy.12 = bf16[1,1,16,128,128]{4,3,2,1,0:T(8,128)(2,1)} copy(bf16[1,1,16,128,128]{4,3,2,1,0:T(8,128)(2,1)} %bitcast.6) | data formatting | bytes 1048576

commit v6 on v5

--- a/solution.py
+++ b/solution.py
@@ -271,8 +271,10 @@
 
         @pl.when(i < 7)
         def _():
-            for j in range(4):
-                to_next(u, (g + j) % 4).start()
+            for flip_z, flip_y in ((1, 1), (0, 1), (1, 0), (0, 0)):
+                z = g // 2 + flip_z * (1 - 2 * (g // 2))
+                y = g % 2 + flip_y * (1 - 2 * (g % 2))
+                to_next(u, z * 2 + y).start()
 
         @pl.when(i > 5)
         def _():
@@ -375,7 +377,7 @@
             dma((8,)), dma((8,)), dma((8,)), dma((8, 2)), dma((8, 2)), dma((8,)), dma((8,)), dma((8,)), dma((8,)),
             dma((9,)), dma,
         ],
-        compiler_params=pltpu.CompilerParams(collective_id=0, has_side_effects=True, vmem_limit_bytes=56 << 20),
+        compiler_params=pltpu.CompilerParams(collective_id=0, has_side_effects=True, vmem_limit_bytes=53 << 20),
         name="sweep",
     )(
         mpo_charge, block_sizes, mpo.reshape(64, 64),

time: 139 us -> 132 us (0.950)
  Pallas kernels: 134 us -> 128 us
  local copies, waits for them, and re-layouts: 5.39 us -> 3.8 us
    pallas_call x1, Pallas kernels: 134 us -> 128 us  [on_device(): pl.pallas_call(kernel, out_shape=jax.ShapeDtypeStruct((UP_VALUES, DOWN_VA...]
    unnamed x3 -> x5, local copies, waits for them, and re-layouts: 4.54 us -> 3.55 us
where the time goes in v6:
time: 132 us
  Pallas kernels  128 us (97%)
  local copies, waits for them, and re-layouts  3.8 us (3%)
    pallas_call x1, Pallas kernels, on_device(): pl.pallas_call(kernel, out_shape=jax.ShapeDtypeStruct((UP_VALUES, DOWN_VA...  128 us
    unnamed x5, local copies, waits for them, and re-layouts  3.55 us

profile of v6, /device:TPU:39, one launch (start us, length us, event | category | flops | bytes accessed | tf_op | source)
XLA Modules:
  0.0 131.5 jit_solution(5770842548830827990)
XLA Ops:
  0.0 0.8 copy.10.charge
  0.8 1.3 copy.9
  2.1 0.2 reshape.15.coeff
  2.3 0.0 copy-start
  2.3 0.7 copy-done
  3.0 127.7 %sweep.1 = bf16[8,2,2,64,128]{4,3,2,1,0:T(8,128)(2,1)S(1)} custom-call(s32[16,2]{1,0:T(8,128)S(1)} %copy.10.charge, s32[9,16]{1,0:T(8,128)S(1)} %copy-done, bf16[64,64]{1,0:T(8,128)(2,1)S(1)} %reshape.15.coeff, bf16[8,2,2,2,2,16,128]{6,5,4,3,2,1,0:T(8,128)(2,1)} %bitcast.9, bf16[4,8,2,128,128]{4,3,2,1,0:T(8,128)(2,1)} %bitcast.7, ...), custom_call_target="tpu_custom_call" | custom-call | tf_op jit(solution)/shard_map/sweep/pallas_call | solution.py:358
  130.7 0.8 copy.12
Async XLA Ops:
  2.3 0.7 copy-start

commit v7 on v6

--- a/solution.py
+++ b/solution.py
@@ -252,6 +252,15 @@
             part_s[u, m] = (own[1, m] + sib_r[u, 1, m].astype(f32)).astype(bf16)
         partial(u).start()
 
+    def give(u, _):
+        for j in range(1, 4):
+            m = (me + j) % 4
+            pltpu.make_async_remote_copy(
+                obuf.at[m, u], out.at[u, d, k], out_ss.at[u], out_rs,
+                device_id=(i, bond_of(g, m)), device_id_type=MESH).start()
+        pltpu.make_async_copy(obuf.at[me, u], out.at[u, d, k], out_ls.at[u]).start()
+        return 0
+
     def finish(u):
         sibling(u, 0).wait_recv()
 
@@ -276,14 +285,9 @@
                 y = g % 2 + flip_y * (1 - 2 * (g % 2))
                 to_next(u, z * 2 + y).start()
 
-        @pl.when(i > 5)
-        def _():
-            for j in range(1, 4):
-                m = (me + j) % 4
-                pltpu.make_async_remote_copy(
-                    obuf.at[m, u], out.at[u, d, k], out_ss.at[u], out_rs,
-                    device_id=(i, bond_of(g, m)), device_id_type=MESH).start()
-            pltpu.make_async_copy(obuf.at[me, u], out.at[u, d, k], out_ls.at[u]).start()
+        @pl.when((i == 7) | ((i == 6) & (u < 4)))
+        def _():
+            give(u, 0)
 
     def step(n, _):
         u, plane = n // 2, n % 2
@@ -311,6 +315,10 @@
         return 0
 
     lax.fori_loop(0, 2 * UP_VALUES, step, 0)
+
+    @pl.when(i == 6)
+    def _():
+        lax.fori_loop(4, UP_VALUES, give, 0)
 
     @pl.when(i < 6)
     def _():

time: 132 us -> 132 us (level)
  no operation moved by 1% of the time
where the time goes in v7:
time: 132 us
  Pallas kernels  128 us (97%)
  local copies, waits for them, and re-layouts  3.8 us (3%)
    pallas_call x1, Pallas kernels, on_device(): pl.pallas_call(kernel, out_shape=jax.ShapeDtypeStruct((UP_VALUES, DOWN_VA...  128 us
    unnamed x5, local copies, waits for them, and re-layouts  3.55 us

profile of v7, /device:TPU:39, one launch (start us, length us, event | category | flops | bytes accessed | tf_op | source)
XLA Modules:
  0.0 131.6 jit_solution(14160911988052502733)
XLA Ops:
  0.0 0.8 copy.10.charge
  0.8 1.3 copy.9
  2.1 0.2 reshape.15.coeff
  2.3 0.0 copy-start
  2.3 0.7 copy-done
  3.0 127.8 %sweep.1 = bf16[8,2,2,64,128]{4,3,2,1,0:T(8,128)(2,1)S(1)} custom-call(s32[16,2]{1,0:T(8,128)S(1)} %copy.10.charge, s32[9,16]{1,0:T(8,128)S(1)} %copy-done, bf16[64,64]{1,0:T(8,128)(2,1)S(1)} %reshape.15.coeff, bf16[8,2,2,2,2,16,128]{6,5,4,3,2,1,0:T(8,128)(2,1)} %bitcast.9, bf16[4,8,2,128,128]{4,3,2,1,0:T(8,128)(2,1)} %bitcast.7, ...), custom_call_target="tpu_custom_call" | custom-call | tf_op jit(solution)/shard_map/sweep/pallas_call | solution.py:366
  130.8 0.8 copy.12
Async XLA Ops:
  2.3 0.7 copy-start

commit v8 on v6

--- a/solution.py
+++ b/solution.py
@@ -272,7 +272,7 @@
         @pl.when(i < 7)
         def _():
             for flip_z, flip_y in ((1, 1), (0, 1), (1, 0), (0, 0)):
-                z = g // 2 + flip_z * (1 - 2 * (g // 2))
+                z = (g // 2 + flip_z + k) % 2
                 y = g % 2 + flip_y * (1 - 2 * (g % 2))
                 to_next(u, z * 2 + y).start()
 

time: 132 us -> 132 us (level)
  no operation moved by 1% of the time
where the time goes in v8:
time: 132 us
  Pallas kernels  128 us (97%)
  local copies, waits for them, and re-layouts  3.8 us (3%)
    pallas_call x1, Pallas kernels, on_device(): pl.pallas_call(kernel, out_shape=jax.ShapeDtypeStruct((UP_VALUES, DOWN_VA...  128 us
    unnamed x5, local copies, waits for them, and re-layouts  3.55 us

profile of v8, /device:TPU:39, one launch (start us, length us, event | category | flops | bytes accessed | tf_op | source)
XLA Modules:
  0.0 131.5 jit_solution(764701141509553961)
XLA Ops:
  0.0 0.8 copy.10.charge
  0.8 1.3 copy.9
  2.1 0.2 reshape.15.coeff
  2.3 0.0 copy-start
  2.3 0.7 copy-done
  3.0 127.7 %sweep.1 = bf16[8,2,2,64,128]{4,3,2,1,0:T(8,128)(2,1)S(1)} custom-call(s32[16,2]{1,0:T(8,128)S(1)} %copy.10.charge, s32[9,16]{1,0:T(8,128)S(1)} %copy-done, bf16[64,64]{1,0:T(8,128)(2,1)S(1)} %reshape.15.coeff, bf16[8,2,2,2,2,16,128]{6,5,4,3,2,1,0:T(8,128)(2,1)} %bitcast.9, bf16[4,8,2,128,128]{4,3,2,1,0:T(8,128)(2,1)} %bitcast.7, ...), custom_call_target="tpu_custom_call" | custom-call | tf_op jit(solution)/shard_map/sweep/pallas_call | solution.py:358
  130.7 0.8 copy.12
Async XLA Ops:
  2.3 0.7 copy-start
